TPU v7x, 256 devices: a whole 4x4x8 slice. The times are simulated.
256 devices in a mesh: prompt: 16 (over z, core), resp: 16 (over x, y).
Axes of the slice: x: 4, y: 4, z: 8, core: 2. Of those that a mesh axis runs over, the one named last changes fastest.
Arguments:
- inputs: bfloat16 [256, 128, 16384], P(('prompt', 'resp')), parts along dimension 0, may hold values from -6 to 6
- cotangent: bfloat16 [256, 128, 16384], P(('prompt', 'resp')), parts along dimension 0, may hold values from -96 to 96
- b_proj: bfloat16 [256, 128, 2048], P(('prompt', 'resp')), parts along dimension 0, may hold values from -0.375 to 0.375
- c_proj: bfloat16 [256, 128, 2048], P(('prompt', 'resp')), parts along dimension 0, may hold values from -0.375 to 0.375
- dt_raw: float32 [256, 128, 256], P(('prompt', 'resp')), parts along dimension 0, may hold values from -6 to 6
- decay_rate: float32 [256], replicated, may hold values from 0.003 to 0.06
- state_codes: bfloat16 [4096, 64, 256], P(('prompt', 'resp')), parts along dimension 0, may hold values from -6 to 6
- state_scales: bfloat16 [4096, 64], P(('prompt', 'resp')), parts along dimension 0, may hold values from 0.25 to 2
- sign_bucket: int32 [256], P(('prompt', 'resp')), parts along dimension 0, may hold values from 0 to 1
- adv_scale: float32 [256], P(('prompt', 'resp')), parts along dimension 0, may hold values from 0.5 to 2
- lengths: int32 [256], P(('prompt', 'resp')), parts along dimension 0, may hold values from 64 to 128, as said below
Outputs:
- grad_state: float32 [4096, 64, 256], P(('prompt', 'resp')), parts along dimension 0
- grad_b: bfloat16 [256, 128, 2048], P(('prompt', 'resp')), parts along dimension 0
- grad_c: bfloat16 [256, 128, 2048], P(('prompt', 'resp')), parts along dimension 0
- grad_dt: float32 [256, 128, 256], P(('prompt', 'resp')), parts along dimension 0
There are 16 independent parts, one for each index of `prompt`. A program takes and returns all parts, laid end to end along the dimension named above; an argument that names none is the same for every part. Nothing has to cross between parts.
Inputs may be any that keep to these rules, and one draw needn't show every extreme that they name: `lengths`: every response has at least 64 valid tokens; some response of each prompt has exactly 128.
All inputs are finite; a program needn't handle non-finite values.
Results may differ from a plain program's by a relative error of at most 0.001.
Values may be sent and summed in bfloat16 or wider, within the bound.
No kernel may reach another device: no remote copies, remote signals or barrier semaphores. Data moves between devices by JAX's collectives and lax.ppermute only.
A program may use at most 128 MiB of HBM per device.

v0:
```python
import jax
import jax.numpy as jnp
from jax import lax
from jax.sharding import PartitionSpec as P


def group_forward(group_x, scores, group_c, group_dt, group_rate, group_state):
    tok_rows = group_x.shape[0]
    head_count = group_dt.shape[1]
    step_size = jax.nn.softplus(group_dt)
    log_decay = jnp.cumsum(-step_size * group_rate[None, :], axis=0)
    decay_rows = log_decay.T
    decay_gap = decay_rows[:, :, None] - decay_rows[:, None, :]
    causal = (
        jnp.arange(tok_rows, dtype=jnp.int32)[:, None]
        >= jnp.arange(tok_rows, dtype=jnp.int32)[None, :]
    )
    attenuation = jnp.where(causal[None], jnp.exp(jnp.where(causal[None], decay_gap, 0.0)), 0.0)
    mixing = attenuation * scores[None] * step_size.T[:, None, :]
    head_x = group_x.reshape(tok_rows, head_count, -1)
    within = jnp.einsum("hts,shp->thp", mixing, head_x, precision=lax.Precision.HIGHEST)
    carried = jnp.exp(log_decay)[:, :, None] * jnp.einsum(
        "tn,hpn->thp", group_c, group_state, precision=lax.Precision.HIGHEST
    )
    return (within + carried).reshape(tok_rows, -1)


def response_grads(x_rows, up_rows, b_rows, c_rows, dt_rows, rate, prefix_state, row_coef):
    state_dim = prefix_state.shape[2]
    head_dim = prefix_state.shape[1]
    group_count = b_rows.shape[1] // state_dim
    group_heads = rate.shape[0] // group_count
    group_width = group_heads * head_dim
    tok_rows = x_rows.shape[0]

    def one_group(group_idx):
        group_x = lax.dynamic_slice_in_dim(x_rows, group_idx * group_width, group_width, 1).astype(
            jnp.float32
        )
        group_dy = (
            lax.dynamic_slice_in_dim(up_rows, group_idx * group_width, group_width, 1).astype(
                jnp.float32
            )
            * row_coef[:, None]
        )
        b_half = lax.dynamic_slice_in_dim(b_rows, group_idx * state_dim, state_dim, 1)
        c_half = lax.dynamic_slice_in_dim(c_rows, group_idx * state_dim, state_dim, 1)
        group_b = b_half.astype(jnp.float32)
        group_c = c_half.astype(jnp.float32)
        scores = jnp.dot(c_half, b_half.T, preferred_element_type=jnp.float32)
        group_dt = lax.dynamic_slice_in_dim(dt_rows, group_idx * group_heads, group_heads, 1)
        group_rate = lax.dynamic_slice_in_dim(rate, group_idx * group_heads, group_heads, 0)
        group_state = lax.dynamic_slice_in_dim(
            prefix_state, group_idx * group_heads, group_heads, 0
        )

        def forward(s_in, c_in, dt_in, state_in):
            return group_forward(group_x, s_in, c_in, dt_in, group_rate, state_in)

        result, pullback = jax.vjp(forward, scores, group_c, group_dt, group_state)
        grads = pullback(group_dy)
        d_scores = grads[0]
        grad_b = jnp.dot(d_scores.T, group_c, precision=lax.Precision.HIGHEST)
        grad_c = jnp.dot(d_scores, group_b, precision=lax.Precision.HIGHEST) + grads[1]
        return (grad_b, grad_c) + tuple(grads[2:])

    results = lax.map(one_group, jnp.arange(group_count, dtype=jnp.int32))
    grad_b = results[0].transpose(1, 0, 2).reshape(tok_rows, -1)
    grad_c = results[1].transpose(1, 0, 2).reshape(tok_rows, -1)
    grad_dt = results[2].transpose(1, 0, 2).reshape(tok_rows, -1)
    return (grad_b, grad_c, grad_dt, results[3].reshape(rate.shape[0], head_dim, state_dim))


def per_device(
    inputs,
    cotangent,
    b_proj,
    c_proj,
    dt_raw,
    decay_rate,
    state_codes,
    state_scales,
    sign_bucket,
    adv_scale,
    lengths,
):
    codes_all, scales_all = (
        lax.all_gather(state_codes, "resp", axis=0, tiled=True),
        lax.all_gather(state_scales, "resp", axis=0, tiled=True),
    )
    prefix_state = codes_all.astype(jnp.float32) * scales_all.astype(jnp.float32)[:, :, None]
    tok_rows = inputs.shape[1]
    sign_value = 2.0 * sign_bucket[0].astype(jnp.float32) - 1.0
    coefficient = sign_value * adv_scale[0] / lengths[0].astype(jnp.float32)
    row_coef = jnp.where(
        jnp.arange(tok_rows, dtype=jnp.int32) < lengths[0], coefficient, jnp.zeros((), jnp.float32)
    )
    grad_b, grad_c, grad_dt, grad_part = response_grads(
        inputs[0], cotangent[0], b_proj[0], c_proj[0], dt_raw[0], decay_rate, prefix_state, row_coef
    )
    grad_state = lax.psum_scatter(grad_part, "resp", scatter_dimension=0, tiled=True)
    return (
        grad_state,
        grad_b.astype(jnp.bfloat16)[None],
        grad_c.astype(jnp.bfloat16)[None],
        grad_dt[None],
    )


def solution(mesh):
    return jax.shard_map(
        per_device,
        mesh=mesh,
        in_specs=(
            P(("prompt", "resp"), None, None),
            P(("prompt", "resp"), None, None),
            P(("prompt", "resp"), None, None),
            P(("prompt", "resp"), None, None),
            P(("prompt", "resp"), None, None),
            P(),
            P(("prompt", "resp"), None, None),
            P(("prompt", "resp"), None),
            P(("prompt", "resp")),
            P(("prompt", "resp")),
            P(("prompt", "resp")),
        ),
        out_specs=(
            P(("prompt", "resp"), None, None),
            P(("prompt", "resp"), None, None),
            P(("prompt", "resp"), None, None),
            P(("prompt", "resp"), None, None),
        ),
        check_vma=False,
    )
```

profile of v0, /device:TPU:130, one launch (start us, length us, event | category | flops | bytes accessed | tf_op | source)
XLA Modules:
  0.0 395.0 jit_solution(7647203711335851857)
XLA Ops:
  9.9 23.7 %all_gather.7 = bf16[256,64]{1,0:T(8,128)(2,1)S(1)} all-gather(bf16[16,64]{1,0:T(8,128)(2,1)} %param.20), channel_id=1, replica_groups=mesh['prompt'=16,'resp'=16] {'resp'}, dimensions={0}, use_global_device_ids=true | all-gather | bytes 34816 | tf_op jit(solution)/shard_map/all_gather | solution.py:89
  33.7 6.4 %copy.55 = bf16[1,128,16384]{1,2,0:T(8,128)(2,1)} copy(bf16[1,128,16384]{2,1,0:T(8,128)(2,1)} %param.13) | data formatting | bytes 8388608 | tf_op args[0]
  40.1 6.4 %copy.54 = bf16[1,128,16384]{1,2,0:T(8,128)(2,1)} copy(bf16[1,128,16384]{2,1,0:T(8,128)(2,1)} %param.14) | data formatting | bytes 8388608 | tf_op args[1]
  46.5 41.2 %all-gather.2.cloned.1.call-done = bf16[256,64,256]{2,1,0:T(8,128)(2,1)} async-done(((bf16[16,64,256]{2,1,0:T(8,128)(2,1)}), bf16[256,64,256]{2,1,0:T(8,128)(2,1)}) %all-gather.2.cloned.1.call-update) | async-done | bytes 8388624 | tf_op jit(solution)/shard_map/all_gather | solution.py:88
  87.7 10.2 %convert_multiply_fusion.1 = f32[256,64,256]{2,1,0:T(8,128)} fusion(bf16[256,64,256]{2,1,0:T(8,128)(2,1)} %all-gather.2.cloned.1.call-done, f32[256,64]{1,0:T(8,128)S(1)} %convert_element_type.54), kind=kLoop, calls=%fused_computation.56 | loop fusion | flops 8388608 | bytes 25231360 | tf_op jit(solution)/shard_map/mul | solution.py:91
  97.9 174.9 %while.17 = (s32[]{:T(128)}, bf16[8,128,256]{2,1,0:T(8,128)(2,1)S(1)}, bf16[8,128,256]{2,1,0:T(8,128)(2,1)S(1)}, f32[8,128,32]{1,2,0:T(8,128)S(1)}, f32[8,32,64,...) while((s32[]{:T(128)}, ...), condition=%wide.region_8.9_spmd.clone, body=%wide.region_0.8_spmd.clone.sunk | while | flops 2938228992 | bytes 15551423 | solution.py:67
  103.8 1.1 convert_multiply_fusion.3
  104.9 3.5 fusion.85
  108.4 2.7 fusion.87
  112.6 3.5 fusion.88
  117.4 2.3 bitcast_dynamic-update-slice_fusion.2
  125.7 1.1 convert_multiply_fusion.3
  126.8 3.5 fusion.85
  130.3 2.7 fusion.87
  133.1 1.1 reduce_window_sum.27
  134.5 3.5 fusion.88
  139.3 2.3 bitcast_dynamic-update-slice_fusion.2
  147.5 1.1 convert_multiply_fusion.3
  148.6 3.5 fusion.85
  152.1 2.7 fusion.87
  156.3 3.5 fusion.88
  161.1 2.3 bitcast_dynamic-update-slice_fusion.2
  169.4 1.1 convert_multiply_fusion.3
  170.5 3.5 fusion.85
  174.0 2.7 fusion.87
  178.2 3.5 fusion.88
  183.0 2.3 bitcast_dynamic-update-slice_fusion.2
  191.2 1.1 convert_multiply_fusion.3
  192.4 3.5 fusion.85
  195.8 2.7 fusion.87
  200.0 3.5 fusion.88
  204.9 2.4 bitcast_dynamic-update-slice_fusion.2
  213.1 1.1 convert_multiply_fusion.3
  214.3 3.5 fusion.85
  217.8 2.7 fusion.87
  222.0 3.5 fusion.88
  226.8 2.3 bitcast_dynamic-update-slice_fusion.2
  235.0 1.1 convert_multiply_fusion.3
  236.1 3.5 fusion.85
  239.6 2.7 fusion.87
  243.8 3.5 fusion.88
  248.6 2.3 bitcast_dynamic-update-slice_fusion.2
  256.9 1.1 convert_multiply_fusion.3
  258.0 3.5 fusion.85
  261.5 2.7 fusion.87
  265.7 3.5 fusion.88
  270.5 2.3 bitcast_dynamic-update-slice_fusion.2
  276.3 111.9 %reduce-scatter.2.cloned.1.call-done = f32[16,64,256]{2,1,0:T(8,128)} async-done(((f32[256,64,256]{2,1,0:T(8,128)}), f32[16,64,256]{2,1,0:T(8,128)}) %reduce-scatter.2.cloned.1.call-update) | async-done | bytes 1048592 | tf_op jit(solution)/shard_map/reduce_scatter | solution.py:101
  (180 shorter events, 57.2 us)
Async XLA Ops:
  7.2 80.5 %all-gather.2.cloned.1.call-start = ((), (), s32[]{:S(2)}) async-start(), calls=%async_computation.1 | async-start | bytes 8912896 | tf_op jit(solution)/shard_map/all_gather | solution.py:88
  7.9 380.2 %reduce-scatter.2.cloned.1.call-start = ((), (), s32[]{:S(2)}) async-start(), calls=%async_computation.2 | async-start | bytes 17825792 | tf_op jit(solution)/shard_map/reduce_scatter | solution.py:101
  46.5 51.4 %copy-start = (bf16[1,128,2048]{2,1,0:T(8,128)(2,1)S(1)}, bf16[1,128,2048]{2,1,0:T(8,128)(2,1)}, u32[]{:S(2)}) copy-start(bf16[1,128,2048]{2,1,0:T(8,128)(2,1)} %param.16) | copy-start | bytes 1572868
  46.5 51.4 %copy-start.1 = (f32[1,128,256]{2,1,0:T(8,128)S(1)}, f32[1,128,256]{2,1,0:T(8,128)}, u32[]{:S(2)}) copy-start(f32[1,128,256]{2,1,0:T(8,128)} %param.17) | copy-start | bytes 393220
  46.5 51.3 %copy-start.2 = (f32[256]{0:T(256)S(1)}, f32[256]{0:T(256)}, u32[]{:S(2)}) copy-start(f32[256]{0:T(256)} %param.18) | copy-start | bytes 3076
Sparse Core Ops, SparseCore 0:
  10.4 77.2 all-gather.1
  273.0 115.1 reduce-scatter.1
where the time goes:
time: 400 us; the launch traced here: 395 us
  waiting for transfers between devices  154 us (38%)
  matrix products  114 us (28%)
  other arithmetic  37.3 us (9%)
  local copies, waits for them, and re-layouts  33.8 us (8%)
  blocking collectives  23.7 us (6%)
  loops' own time  16.3 us (4%)
  between operations  16.1 us (4%)
    reduce_scatter x1, waiting for transfers between devices, per_device(): lax.psum_scatter(grad_part, 'resp', scatter_dimension=0, tiled=True)  112 us
    dot_general x24, matrix products, group_forward(): jnp.einsum('tn,hpn->thp', group_c, group_state, precision=lax.Precision.H...  67.7 us
    all_gather x1, waiting for transfers between devices, per_device(): lax.all_gather(state_codes, 'resp', axis=0, tiled=True)  41.2 us
    dot_general x8, matrix products, group_forward(): jnp.einsum('hts,shp->thp', mixing, head_x, precision=lax.Precision.HIGHEST)  27.8 us
    all_gather x1, blocking collectives, per_device(): lax.all_gather(state_scales, 'resp', axis=0, tiled=True)  23.7 us
    another operation x1, loops' own time, response_grads(): results = lax.map(one_group, jnp.arange(group_count, dtype=jnp.int32))  16.3 us
    unnamed x9, local copies, waits for them, and re-layouts  13.5 us
    another operation x16, other arithmetic, group_forward(): log_decay = jnp.cumsum(-step_size * group_rate[None, :], axis=0)  10.4 us
  transfers between devices with their start and end apart: 2, of which 2 were waited for; matrix products, arithmetic and copies ran while one was open for 4% of the time, Pallas kernels for 0%

commit v1 on v0

v1 whole, which is shorter than its diff:
```python
import functools

import jax
import jax.numpy as jnp
from jax import lax
from jax.experimental import pallas as pl
from jax.experimental.pallas import tpu as pltpu
from jax.sharding import Mesh, PartitionSpec as P

F32 = jnp.float32
BF16 = jnp.bfloat16

TOK = 128
H = 256
PS = 64
N = 256
G = 8
ROW = 4
RH = H // ROW
OH = RH // ROW
CH = OH // 2
CW = CH * PS
OW = OH * PS
RW = RH * PS
PW = ROW * CW
PACK0 = PW + 2 * N + 2 * RH
MIB = 1024 * 1024


def dot(a, b):
    return lax.dot_general(a, b, (((1,), (0,)), ((), ())), preferred_element_type=F32)


def dot_nt(a, b):
    return lax.dot_general(a, b, (((1,), (1,)), ((), ())), preferred_element_type=F32)


def dot_tn(a, b):
    return lax.dot_general(a, b, (((0,), (0,)), ((), ())), preferred_element_type=F32)


def split2(a):
    hi = a.astype(BF16)
    lo = (a - hi.astype(F32)).astype(BF16)
    return hi, lo


def split3(a):
    hi = a.astype(BF16)
    rest = a - hi.astype(F32)
    mid = rest.astype(BF16)
    lo = (rest - mid.astype(F32)).astype(BF16)
    return hi, mid, lo


def iota(shape, dim):
    return lax.broadcasted_iota(jnp.int32, shape, dim)


def softplus(a):
    return jnp.maximum(a, 0.0) + jnp.log1p(jnp.exp(-jnp.abs(a)))


def prep_kernel(
    x_idx, sign, adv, length, dt_ref, rate_ref, scale_ref, cot_hbm, c_hbm, codes_hbm, *rest
):
    packs0, packs1 = rest[0:4], rest[4:8]
    stp, ep_ref, fp_ref, sc_ref, sems = rest[8:13]
    me = x_idx[0]
    copies = []

    def start(src, dst):
        copy = pltpu.make_async_copy(src, dst, sems.at[len(copies)])
        copy.start()
        copies.append(copy)

    start(codes_hbm, stp.at[pl.ds(0, OW)])
    for k in (2, 1, 3, 0):
        there = lax.rem(me + k, ROW)
        for j in range(ROW):
            at = pl.multiple_of(there * RW + j * OW, CW)
            start(cot_hbm.at[0, :, pl.ds(at, CW)], packs0[k].at[:, pl.ds(j * CW, CW)])
        at = pl.multiple_of(there * 2 * N, 2 * N)
        start(c_hbm.at[0, :, pl.ds(at, 2 * N)], packs0[k].at[:, pl.ds(PW, 2 * N)])
    for k in (2, 1, 3, 0):
        there = lax.rem(me + k, ROW)
        for j in range(ROW):
            at = pl.multiple_of(there * RW + j * OW + CW, CW)
            start(cot_hbm.at[0, :, pl.ds(at, CW)], packs1[k].at[:, pl.ds(j * CW, CW)])

    step = softplus(dt_ref[0])
    tri = (iota((TOK, TOK), 0) >= iota((TOK, TOK), 1)).astype(F32).astype(BF16)
    s_hi, s_mid, s_lo = split3(step)
    total = dot(tri, s_hi) + dot(tri, s_mid) + dot(tri, s_lo)
    log_decay = -rate_ref[...] * total
    weight = (2.0 * sign[0].astype(F32) - 1.0) * adv[0] / jnp.full((TOK, H), length[0], jnp.int32).astype(F32)
    weight = jnp.where(iota((TOK, H), 0) < length[0], weight, 0.0)
    e_hi, e_lo = split2(weight * jnp.exp(log_decay))
    f_hi, f_lo = split2(step * jnp.exp(-log_decay))
    for q in range(ROW):
        cols = slice(q * RH, (q + 1) * RH)
        ep_ref[q] = jnp.concatenate([e_hi[:, cols], e_lo[:, cols]], axis=1)
        fp_ref[q] = jnp.concatenate([f_hi[:, cols], f_lo[:, cols]], axis=1)

    scale = scale_ref[...].astype(F32)
    two = jnp.concatenate([scale, scale], axis=1)
    tiled = jnp.concatenate([two] * (OW // 128), axis=1)
    own = iota((OH, OW), 0) == iota((OH, OW), 1) // PS
    row = dot(jnp.ones((OH, OH), BF16), jnp.where(own, tiled, 0.0).astype(BF16))
    held = jnp.zeros((OH, N), F32)
    for q in range(OW // N):
        held = jnp.where(iota((OH, N), 0) == q, row[:, q * N : (q + 1) * N], held)
    sc_ref[...] = held.astype(BF16)
    start(sc_ref, stp.at[pl.ds(OW, OH)])
    for k in (2, 1, 3, 0):
        there = lax.rem(me + k, ROW)
        start(ep_ref.at[there], packs0[k].at[:, pl.ds(PW + 2 * N, 2 * RH)])
    for copy in copies:
        copy.wait()


def prep(x_idx, sign, adv, length, dt, rate, scales, cot, c, codes):
    any_spec = pl.BlockSpec(memory_space=pl.ANY)
    smem = pl.BlockSpec(memory_space=pltpu.SMEM)
    vmem = pl.BlockSpec(memory_space=pltpu.VMEM)
    outs = pl.pallas_call(
        prep_kernel,
        out_shape=[jax.ShapeDtypeStruct((TOK, PACK0), BF16)] * 4
        + [jax.ShapeDtypeStruct((TOK, PW), BF16)] * 4
        + [jax.ShapeDtypeStruct((OW + OH, N), BF16)]
        + [jax.ShapeDtypeStruct((ROW, TOK, 2 * RH), BF16)] * 2,
        in_specs=[smem] * 4 + [vmem] * 3 + [any_spec] * 3,
        out_specs=[any_spec] * 9 + [vmem] * 2,
        scratch_shapes=[pltpu.VMEM((OH, N), BF16), pltpu.SemaphoreType.DMA((48,))],
        compiler_params=pltpu.CompilerParams(vmem_limit_bytes=16 * MIB),
        name="prep",
    )(x_idx, sign, adv, length, dt, rate, scales, cot, c, codes)
    return outs[0:4], outs[4:8], outs[8], outs[9], outs[10]


def within_kernel(x_ref, cot_ref, b_ref, c_ref, ep_ref, fp_ref, gb_ref, gc_ref, q_ref, sr_ref, sel_ref):
    g = pl.program_id(0)
    width = H // G * PS

    @pl.when(g == 0)
    def _():
        for half in range(2):
            row = iota((2 * RH, width), 0)
            head = iota((2 * RH, width), 1) // PS + half * (H // G)
            hit = (row == head) | (row == head + RH)
            sel_ref[half] = jnp.where(hit, 1.0, 0.0).astype(BF16)

    parity = lax.rem(g, 2)
    sel = sel_ref[parity]
    wide = dot(jnp.concatenate([ep_ref[0], fp_ref[0]], axis=0), sel)
    dy = cot_ref[0].astype(F32) * wide[:TOK]
    xs = x_ref[0].astype(F32) * wide[TOK:]
    d_hi, d_lo = split2(dy)
    x_hi, x_lo = split2(xs)
    b, c = b_ref[0], c_ref[0]
    rows, cols = iota((TOK, TOK), 0), iota((TOK, TOK), 1)
    s_hi, s_lo = split2(jnp.where(rows >= cols, dot_nt(c, b), 0.0))
    t_hi, t_lo = split2(jnp.where(rows <= cols, dot_nt(b, c), 0.0))
    d_two = jnp.concatenate([d_hi, d_lo], axis=0)
    x_two = jnp.concatenate([x_hi, x_lo], axis=0)
    y = dot(jnp.concatenate([s_hi, s_hi], axis=1), x_two) + dot(s_lo, x_hi)
    z = dot(jnp.concatenate([t_hi, t_hi], axis=1), d_two) + dot(t_lo, d_hi)
    ds4 = dot_nt(d_two, x_two)
    ds = ds4[:TOK, :TOK] + ds4[:TOK, TOK:] + ds4[TOK:, :TOK] + ds4[TOK:, TOK:]
    ds = jnp.where(rows >= cols, ds, 0.0)
    gb_ref[0] = dot(
        jnp.concatenate(split2(ds.T), axis=1), jnp.concatenate([c, c], axis=0)
    ).astype(BF16)
    gc_ref[...] = dot(jnp.concatenate(split2(ds), axis=1), jnp.concatenate([b, b], axis=0))
    q_hi, q_lo = split2(dy * y)
    r_hi, r_lo = split2(xs * z)
    seg = dot_nt(jnp.concatenate([q_hi, q_lo, r_hi, r_lo], axis=0), sel)
    q = seg[:TOK] + seg[TOK : 2 * TOK]
    sr = seg[2 * TOK : 3 * TOK] + seg[3 * TOK :]

    @pl.when(parity == 0)
    def _():
        q_ref[0] = q
        sr_ref[0] = sr

    @pl.when(parity == 1)
    def _():
        q_ref[0] += q
        sr_ref[0] += sr


def within(x, cot, b, c, ep, fp):
    width = H // G * PS
    wide = pl.BlockSpec((1, TOK, width), lambda g: (0, 0, g))
    narrow = pl.BlockSpec((1, TOK, N), lambda g: (0, 0, g))
    pair = pl.BlockSpec((1, TOK, 2 * RH), lambda g: (g // 2, 0, 0))
    return pl.pallas_call(
        within_kernel,
        grid=(G,),
        out_shape=[
            jax.ShapeDtypeStruct((1, TOK, G * N), BF16),
            jax.ShapeDtypeStruct((TOK, G * N), F32),
            jax.ShapeDtypeStruct((ROW, TOK, 2 * RH), F32),
            jax.ShapeDtypeStruct((ROW, TOK, 2 * RH), F32),
        ],
        in_specs=[wide, wide, narrow, narrow, pair, pair],
        out_specs=[narrow, pl.BlockSpec((TOK, N), lambda g: (0, g)), pair, pair],
        scratch_shapes=[pltpu.VMEM((2, 2 * RH, width), BF16)],
        compiler_params=pltpu.CompilerParams(vmem_limit_bytes=40 * MIB),
        cost_estimate=pl.CostEstimate(
            flops=12_000_000_000, bytes_accessed=12 * MIB, transcendentals=0
        ),
        name="within",
    )(x, cot, b, c, ep, fp)


def owner_kernel(chunk, *refs):
    cots, cs, es = refs[0:4], refs[4:8], refs[8:12]
    codes_ref, sc_ref = refs[12:14]
    olds = refs[14:18] if chunk else None
    outs = refs[18:] if chunk else refs[14:]
    gs_ref, rets = outs[0], outs[1:5]
    j = pl.program_id(0)

    @pl.when(j == 0)
    def _():
        for k in range(ROW):
            rets[k][...] = olds[k][...] if chunk else jnp.zeros_like(rets[k])

    cot = jnp.concatenate([r[...] for r in cots], axis=0).astype(F32)
    c = jnp.concatenate([r[...] for r in cs], axis=0)
    e = jnp.concatenate([r[...] for r in es], axis=0)
    held = sc_ref[0].astype(F32)
    at = chunk * CW // N
    scale = jnp.concatenate([held[at : at + 1], held[at + 1 : at + 2]], axis=1)
    row = iota((2 * RH, CW), 0)
    head = iota((2 * RH, CW), 1) // PS + j * OH + chunk * CH
    hit = (row == head) | (row == head + RH)
    sel = jnp.where(hit, 1.0, 0.0).astype(BF16)
    sel_scaled = jnp.where(hit, jnp.broadcast_to(scale, hit.shape), 0.0).astype(BF16)
    dy = cot * dot(e, sel_scaled)
    d_hi, d_lo = split2(dy)
    codes = codes_ref[0]
    gs_ref[0] = dot_tn(c, d_hi) + dot_tn(c, d_lo)
    gc = dot(d_hi, codes) + dot(d_lo, codes)
    p_hi, p_lo = split2(dy * dot_nt(c, codes))
    q = dot_nt(p_hi, sel) + dot_nt(p_lo, sel)
    for k in range(ROW):
        rets[k][:, 2 * N :] += q[k * TOK : (k + 1) * TOK]

    @pl.when(j < ROW // 2)
    def _():
        for k in range(ROW):
            rets[k][:, :N] += gc[k * TOK : (k + 1) * TOK]

    @pl.when(j >= ROW // 2)
    def _():
        for k in range(ROW):
            rets[k][:, N : 2 * N] += gc[k * TOK : (k + 1) * TOK]


def owner(chunk, cots, packs0, states, olds):
    cot_spec = pl.BlockSpec((TOK, CW), lambda j: (0, j))
    c_spec = pl.BlockSpec((TOK, N), lambda j: (0, PW // N + j // 2))
    e_spec = pl.BlockSpec((TOK, 2 * RH), lambda j: (0, (PW + 2 * N) // (2 * RH)))
    ret_spec = pl.BlockSpec((TOK, 2 * N + 2 * RH), lambda j: (0, 0))
    ret_shape = jax.ShapeDtypeStruct((TOK, 2 * N + 2 * RH), F32)
    outs = pl.pallas_call(
        functools.partial(owner_kernel, chunk),
        grid=(ROW,),
        out_shape=[jax.ShapeDtypeStruct((ROW, N, CW), F32)] + [ret_shape] * 4,
        in_specs=[cot_spec] * 4
        + [c_spec] * 4
        + [e_spec] * 4
        + [
            pl.BlockSpec((1, CW, N), lambda j: (j, chunk, 0)),
            pl.BlockSpec((1, OH, N), lambda j: (j, OW // OH, 0)),
        ]
        + [ret_spec] * (4 if chunk else 0),
        out_specs=[pl.BlockSpec((1, N, CW), lambda j: (j, 0, 0))] + [ret_spec] * 4,
        compiler_params=pltpu.CompilerParams(vmem_limit_bytes=40 * MIB),
        cost_estimate=pl.CostEstimate(
            flops=4_000_000_000, bytes_accessed=8 * MIB, transcendentals=0
        ),
        name=f"owner{chunk}",
    )(*cots, *packs0, *packs0, states, states, *(olds if chunk else ()))
    return outs[0], outs[1:]


def tokens_kernel(x_idx, dt_ref, rate_ref, gc_ref, q_ref, sr_ref, r0, r1, r2, r3, out_gc, out_dt):
    me = x_idx[0]
    lane = iota((TOK, H), 1) // RH
    q = jnp.zeros((TOK, H), F32)
    for k, ret in enumerate((r0, r1, r2, r3)):
        there = lax.rem(me + k, ROW)
        cols = pl.ds(pl.multiple_of(there * 2 * N, 2 * N), 2 * N)
        out_gc[0, :, cols] = (gc_ref[:, cols] + ret[:, : 2 * N]).astype(BF16)
        held = ret[:, 2 * N :]
        q = jnp.where(lane == there, jnp.concatenate([held, held], axis=1), q)
    sr = jnp.zeros((TOK, H), F32)
    for b in range(ROW):
        q = q + jnp.where(lane == b, jnp.concatenate([q_ref[b]] * 2, axis=1), 0.0)
        sr = sr + jnp.where(lane == b, jnp.concatenate([sr_ref[b]] * 2, axis=1), 0.0)
    dt = dt_ref[0]
    step = softplus(dt)
    tri = (iota((TOK, TOK), 0) <= iota((TOK, TOK), 1)).astype(F32).astype(BF16)
    a_hi, a_mid, a_lo = split3(q - sr)
    tail = dot(tri, a_hi) + dot(tri, a_mid) + dot(tri, a_lo)
    d_step = sr / step - rate_ref[...] * tail
    out_dt[0] = d_step / (1.0 + jnp.exp(-dt))


def tokens(x_idx, dt, rate, gc, q, sr, rets):
    smem = pl.BlockSpec(memory_space=pltpu.SMEM)
    vmem = pl.BlockSpec(memory_space=pltpu.VMEM)
    return pl.pallas_call(
        tokens_kernel,
        out_shape=[
            jax.ShapeDtypeStruct((1, TOK, G * N), BF16),
            jax.ShapeDtypeStruct((1, TOK, H), F32),
        ],
        in_specs=[smem] + [vmem] * 9,
        out_specs=[vmem] * 2,
        compiler_params=pltpu.CompilerParams(vmem_limit_bytes=24 * MIB),
        name="tokens",
    )(x_idx, dt, rate, gc, q, sr, *rets)


def state_kernel(a_ref, b_ref, sc_ref, out_ref):
    held = sc_ref[...].astype(F32)
    for chunk, ref in enumerate((a_ref, b_ref)):
        at = chunk * CW // N
        scale = jnp.concatenate([held[at : at + 1], held[at + 1 : at + 2]], axis=1)
        out_ref[pl.ds(chunk * CW, CW), :] = (ref[0] / scale).T


def state_out(a, b, stp):
    block = pl.BlockSpec((1, N, CW), lambda i: (0, 0, 0))
    return pl.pallas_call(
        state_kernel,
        grid=(1,),
        out_shape=jax.ShapeDtypeStruct((OW, N), F32),
        in_specs=[block, block, pl.BlockSpec((OH, N), lambda i: (OW // OH, 0))],
        out_specs=pl.BlockSpec((OW, N), lambda i: (0, 0)),
        compiler_params=pltpu.CompilerParams(vmem_limit_bytes=16 * MIB),
        name="state_out",
    )(a, b, stp)


def shift(k):
    return [(i, (i + k) % ROW) for i in range(ROW)]


def per_device(
    inputs, cotangent, b_proj, c_proj, dt_raw, decay_rate, state_codes, state_scales, sign, adv, lengths
):
    x_idx = lax.axis_index("rx").astype(jnp.int32)[None]
    rate = decay_rate[None]
    packs0, packs1, stp, ep, fp = prep(
        x_idx, sign, adv, lengths, dt_raw, rate, state_scales, cotangent, c_proj,
        state_codes.reshape(OW, N),
    )
    states = lax.all_gather(stp[None], "ry", axis=0, tiled=True)

    def exchange(packs):
        return [packs[0]] + [lax.ppermute(packs[k], "rx", shift(k)) for k in (1, 2, 3)]

    got0 = exchange(packs0)
    got1 = exchange(packs1)
    grad_b, gc_part, q, sr = within(inputs, cotangent, b_proj, c_proj, ep, fp)
    gs0, rets0 = owner(0, got0, got0, states, None)
    red0 = lax.psum_scatter(gs0, "ry", scatter_dimension=0, tiled=True)
    gs1, rets1 = owner(1, got1, got0, states, rets0)
    red1 = lax.psum_scatter(gs1, "ry", scatter_dimension=0, tiled=True)
    back = [rets1[0]] + [lax.ppermute(rets1[k], "rx", shift(-k)) for k in (1, 2, 3)]
    grad_c, grad_dt = tokens(x_idx, dt_raw, rate, gc_part, q, sr, back)
    grad_state = state_out(red0, red1, stp)
    return grad_state.reshape(OH, PS, N), grad_b, grad_c, grad_dt


def solution(mesh):
    prompts = mesh.shape["prompt"]
    mesh3 = Mesh(mesh.devices.reshape(prompts, ROW, ROW), ("prompt", "rx", "ry"))
    split = ("prompt", "rx", "ry")
    three = P(split, None, None)
    return jax.shard_map(
        per_device,
        mesh=mesh3,
        in_specs=(three,) * 5 + (P(), three, P(split, None)) + (P(split),) * 3,
        out_specs=(three,) * 4,
        check_vma=False,
    )
```

time: 400 us -> 169 us (0.42)
  matrix products: 114 us -> 0 us
  waiting for transfers between devices: 154 us -> 50.2 us
  Pallas kernels: 0 us -> 45.4 us
  other arithmetic: 37.3 us -> 0 us
  blocking collectives: 23.7 us -> 0 us
  loops' own time: 16.3 us -> 0 us
  starting transfers between devices: 0.08 us -> 14.4 us
  local copies, waits for them, and re-layouts: 33.8 us -> 40.5 us
    dot_general x56 -> x0, matrix products: 114 us -> none  [the longest x24 67.7 us: group_forward(): jnp.einsum('tn,hpn->thp', group_c, group_state, precision=lax.Precision.H...]
    reduce_scatter x1 -> x2, waiting for transfers between devices: 112 us -> 0.01 us  [the longest x1 0.01 us: per_device(): red0 = lax.psum_scatter(gs0, 'ry', scatter_dimension=0, tiled=True)]
    ppermute x0 -> x9, waiting for transfers between devices: none -> 49.8 us  [the longest x6 49.8 us: exchange(): lax.ppermute(packs[k], 'rx', shift(k))]
    pallas_call x0 -> x6, Pallas kernels: none -> 45.4 us  [the longest x1 24.6 us: within(): pl.pallas_call(within_kernel, grid=(G,), out_shape=[jax.ShapeDtypeStruct(...]
    all_gather x1, waiting for transfers between devices: 41.2 us -> 0.37 us  [per_device(): states = lax.all_gather(stp[None], 'ry', axis=0, tiled=True)]
    unnamed x9 -> x92, local copies, waits for them, and re-layouts: 13.5 us -> 40.5 us
    all_gather x1 -> x0, blocking collectives: 23.7 us -> none  [per_device(): lax.all_gather(state_scales, 'resp', axis=0, tiled=True)]
    mul x17 -> x0, other arithmetic: 20.3 us -> none  [the longest x1 10.2 us: per_device(): codes_all.astype(jnp.float32) * scales_all.astype(jnp.float32)[:, :, None]]
  transfers between devices with their start and end apart: 2 -> 12, of which waited for: 2 -> 7; matrix products, arithmetic and copies ran while one was open for 4% -> 0% of each run, Pallas kernels for 0% -> 20%
where the time goes in v1:
time: 169 us; the launch traced here: 166 us
  waiting for transfers between devices  50.2 us (30%)
  Pallas kernels  45.4 us (27%)
  local copies, waits for them, and re-layouts  40.5 us (24%)
  between operations  15.8 us (9%)
  starting transfers between devices  14.4 us (9%)
    ppermute x6, waiting for transfers between devices, exchange(): lax.ppermute(packs[k], 'rx', shift(k))  49.8 us
    unnamed x92, local copies, waits for them, and re-layouts  40.5 us
    pallas_call x1, Pallas kernels, within(): pl.pallas_call(within_kernel, grid=(G,), out_shape=[jax.ShapeDtypeStruct(...  24.6 us
    pallas_call x2, Pallas kernels, owner(): pl.pallas_call(functools.partial(owner_kernel, chunk), grid=(ROW,), out_s...  15.6 us
    ppermute x6, starting transfers between devices, exchange(): lax.ppermute(packs[k], 'rx', shift(k))  9.62 us
    ppermute x3, starting transfers between devices, per_device(): lax.ppermute(rets1[k], 'rx', shift(-k))  4.7 us
  transfers between devices with their start and end apart: 12, of which 7 were waited for; matrix products, arithmetic and copies ran while one was open for 0% of the time, Pallas kernels for 20%

profile of v1, /device:TPU:130, one launch (start us, length us, event | category | flops | bytes accessed | tf_op | source)
XLA Modules:
  0.0 166.4 jit_solution(11950383344849049847)
XLA Ops:
  9.2 2.2 %copy-done = bf16[1,128,16384]{2,1,0:T(8,128)(2,1)S(1)} copy-done((bf16[1,128,16384]{2,1,0:T(8,128)(2,1)S(1)}, bf16[1,128,16384]{2,1,0:T(8,128)(2,1)}, u32[]{:S(2)}) %copy-start) | copy-done | bytes 4194328
  11.3 1.0 copy-done.2
  12.4 1.0 copy-done.3
  13.4 0.9 copy-done.7
  15.7 2.1 %prep.1 = (bf16[128,2688]{1,0:T(8,128)(2,1)S(1)}, bf16[128,2688]{1,0:T(8,128)(2,1)S(1)}, bf16[128,2688]{1,0:T(8,128)(2,1)S(1)}, bf16[128,2688]{1,0:T(8,128)(2,1)...) custom-call(s32[1]{0:T(128)} %bitcast.x_idx, ...), custom_call_target="tpu_custom_call" | custom-call | tf_op jit(solution)/shard_map/prep/pallas_call | solution.py:126
  18.6 0.8 copy-done.29
  21.6 1.6 collective-permute-start
  23.2 1.1 collective-permute-start.1
  24.3 2.2 %collective-permute-start.2 = (bf16[128,2688]{1,0:T(8,128)(2,1)S(1)}, bf16[128,2688]{1,0:T(8,128)(2,1)S(1)}, u32[]{:S(2)}, u32[]{:S(2)}) collective-permute-start(bf16[128,2688]{1,0:T(8,128)(2,1)S(1)} %get-tuple-element.34), channel_id=1, source_target_pairs={{0,12},{4,0},{8,4},{12,8},{1,13},{5,1},{9,5},{13,9},{2,14},{6,2},{... | collective-permute-start | bytes 2064392 | tf_op jit(solution)/shard_map/ppermute | solution.py:366
  26.5 13.6 %collective-permute-done.refs_1_.refs_5_.refs_9_ = bf16[128,2688]{1,0:T(8,128)(2,1)S(1)} collective-permute-done((bf16[128,2688]{1,0:T(8,128)(2,1)S(1)}, bf16[128,2688]{1,0:T(8,128)(2,1)S(1)}, u32[]{:S(2)}, u32[]{:S(2)}) %collective-permute-start) | collective-permute-done | bytes 688160 | tf_op jit(solution)/shard_map/ppermute | solution.py:366
  40.0 0.8 copy-done.17
  40.9 2.2 %collective-permute-done.1.refs_2_.refs_6_.refs_10_ = bf16[128,2688]{1,0:T(8,128)(2,1)S(1)} collective-permute-done((bf16[128,2688]{1,0:T(8,128)(2,1)S(1)}, bf16[128,2688]{1,0:T(8,128)(2,1)S(1)}, u32[]{:S(2)}, u32[]{:S(2)}) %collective-permute-start.1) | collective-permute-done | bytes 688160 | tf_op jit(solution)/shard_map/ppermute | solution.py:366
  43.1 0.9 copy-done.20
  43.9 11.7 %collective-permute-done.2.refs_3_.refs_7_.refs_11_ = bf16[128,2688]{1,0:T(8,128)(2,1)S(1)} collective-permute-done((bf16[128,2688]{1,0:T(8,128)(2,1)S(1)}, bf16[128,2688]{1,0:T(8,128)(2,1)S(1)}, u32[]{:S(2)}, u32[]{:S(2)}) %collective-permute-start.2) | collective-permute-done | bytes 688160 | tf_op jit(solution)/shard_map/ppermute | solution.py:366
  55.7 0.9 copy-done.23
  56.9 1.6 copy-done.13
  58.5 1.1 copy-done.18
  59.6 1.1 copy-done.21
  60.7 1.1 copy-done.24
  61.8 8.0 %owner0.1 = (f32[4,256,512]{2,1,0:T(8,128)}, f32[128,640]{1,0:T(8,128)S(1)}, f32[128,640]{1,0:T(8,128)S(1)}, f32[128,640]{1,0:T(8,128)S(1)}, f32[128,640]{1,0:T(8,128)S(1)}) custom-call(bf16[128,2688]{1,0:T(8,128)(2,1)S(1)} %get-tuple-element.31.refs_0_.refs_4_.refs_8_, bf16[128,2688]{1,0:T(8,128)(2,1)S(1)} %copy-done.18, bf16[128,2688]{1,0:T(8,128)(2,1)S(1)} %copy-done.21, ...), custom_call_target="tpu_custom_call" | custom-call | flops 4000000000 | bytes 8388608 | tf_op jit(solution)/shard_map/owner0/pallas_call | solution.py:268
  72.9 1.5 collective-permute-start.3
  74.4 1.8 %collective-permute-start.4 = (bf16[128,2048]{1,0:T(8,128)(2,1)}, bf16[128,2048]{1,0:T(8,128)(2,1)S(1)}, u32[]{:S(2)}, u32[]{:S(2)}) collective-permute-start(bf16[128,2048]{1,0:T(8,128)(2,1)} %copy-done.29), channel_id=1, source_target_pairs={{0,8},{4,12},{8,0},{12,4},{1,9},{5,13},{9,1},{13,5},{2,10},{6,14},... | collective-permute-start | bytes 1572872 | tf_op jit(solution)/shard_map/ppermute | solution.py:366
  76.2 1.5 collective-permute-start.5
  77.7 10.3 %collective-permute-done.3.refs_1_ = bf16[128,2048]{1,0:T(8,128)(2,1)S(1)} collective-permute-done((bf16[128,2048]{1,0:T(8,128)(2,1)}, bf16[128,2048]{1,0:T(8,128)(2,1)S(1)}, u32[]{:S(2)}, u32[]{:S(2)}) %collective-permute-start.3) | collective-permute-done | bytes 524320 | tf_op jit(solution)/shard_map/ppermute | solution.py:366
  88.0 3.0 %collective-permute-done.4.refs_2_ = bf16[128,2048]{1,0:T(8,128)(2,1)S(1)} collective-permute-done((bf16[128,2048]{1,0:T(8,128)(2,1)}, bf16[128,2048]{1,0:T(8,128)(2,1)S(1)}, u32[]{:S(2)}, u32[]{:S(2)}) %collective-permute-start.4) | collective-permute-done | bytes 524320 | tf_op jit(solution)/shard_map/ppermute | solution.py:366
  91.0 8.9 %collective-permute-done.5.refs_3_ = bf16[128,2048]{1,0:T(8,128)(2,1)S(1)} collective-permute-done((bf16[128,2048]{1,0:T(8,128)(2,1)S(1)}, bf16[128,2048]{1,0:T(8,128)(2,1)S(1)}, u32[]{:S(2)}, u32[]{:S(2)}) %collective-permute-start.5) | collective-permute-done | bytes 524320 | tf_op jit(solution)/shard_map/ppermute | solution.py:366
  99.9 1.1 copy-done.16
  101.0 1.1 copy-done.19
  102.1 1.1 copy-done.22
  103.2 1.1 copy-done.25
  104.3 1.1 copy-done.28
  105.4 1.0 copy-done.39
  106.4 1.0 copy-done.41
  107.3 1.0 copy-done.43
  108.3 1.0 copy-done.45
  109.3 7.6 %owner1.1 = (f32[4,256,512]{2,1,0:T(8,128)}, f32[128,640]{1,0:T(8,128)S(1)}, f32[128,640]{1,0:T(8,128)S(1)}, f32[128,640]{1,0:T(8,128)S(1)}, f32[128,640]{1,0:T(8,128)S(1)}) custom-call(bf16[128,2048]{1,0:T(8,128)(2,1)S(1)} %copy-done.28, bf16[128,2048]{1,0:T(8,128)(2,1)S(1)} %collective-permute-done.3.refs_1_, ...), custom_call_target="tpu_custom_call" | custom-call | flops 4000000000 | bytes 8388608 | tf_op jit(solution)/shard_map/owner1/pallas_call | solution.py:268
  119.1 0.9 collective-permute-start.6
  120.0 2.1 %collective-permute-start.7 = (f32[128,640]{1,0:T(8,128)}, f32[128,640]{1,0:T(8,128)S(1)}, u32[]{:S(2)}, u32[]{:S(2)}) collective-permute-start(f32[128,640]{1,0:T(8,128)} %copy-done.32), channel_id=1, source_target_pairs={{0,8},{4,12},{8,0},{12,4},{1,9},{5,13},{9,1},{13,5},{2,10},{6,14},... | collective-permute-start | bytes 983048 | tf_op jit(solution)/shard_map/ppermute | solution.py:375
  122.1 1.7 %collective-permute-start.8 = (f32[128,640]{1,0:T(8,128)}, f32[128,640]{1,0:T(8,128)S(1)}, u32[]{:S(2)}, u32[]{:S(2)}) collective-permute-start(f32[128,640]{1,0:T(8,128)} %copy-done.31), channel_id=1, source_target_pairs={{0,4},{4,8},{8,12},{12,0},{1,5},{5,9},{9,13},{13,1},{2,6},{6,10},{... | collective-permute-start | bytes 983048 | tf_op jit(solution)/shard_map/ppermute | solution.py:375
  123.8 2.2 %copy-done.1 = bf16[1,128,16384]{2,1,0:T(8,128)(2,1)S(1)} copy-done((bf16[1,128,16384]{2,1,0:T(8,128)(2,1)S(1)}, bf16[1,128,16384]{2,1,0:T(8,128)(2,1)}, u32[]{:S(2)}) %copy-start.1) | copy-done | bytes 4194328
  126.0 2.2 %copy-done.12 = bf16[1,128,16384]{2,1,0:T(8,128)(2,1)S(1)} copy-done((bf16[1,128,16384]{2,1,0:T(8,128)(2,1)S(1)}, bf16[1,128,16384]{2,1,0:T(8,128)(2,1)}, u32[]{:S(2)}) %copy-start.12) | copy-done | bytes 4194328
  128.2 0.9 copy-done.35
  129.1 0.9 copy-done.37
  130.0 24.6 %within.1 = (bf16[1,128,2048]{2,1,0:T(8,128)(2,1)}, f32[128,2048]{1,0:T(8,128)S(1)}, f32[4,128,128]{2,1,0:T(8,128)S(1)}, f32[4,128,128]{2,1,0:T(8,128)S(1)}) custom-call(bf16[1,128,16384]{2,1,0:T(8,128)(2,1)S(1)} %copy-done.12, bf16[1,128,16384]{2,1,0:T(8,128)(2,1)S(1)} %copy-done.1, bf16[1,128,2048]{2,1,0:T(8,128)(2,1)S(1)} %copy-done.26, ...), custom_call_target="tpu_custom_call" | custom-call | flops 12000000000 | bytes 12582912 | tf_op jit(solution)/shard_map/within/pallas_call | solution.py:197
  154.6 1.2 tokens.1
  155.8 1.0 copy-done.5
  156.8 1.0 copy-done.6
  157.8 2.0 %state_out.1 = f32[1024,256]{1,0:T(8,128)} custom-call(f32[1,256,512]{2,1,0:T(8,128)S(1)} %copy-done.5, f32[1,256,512]{2,1,0:T(8,128)S(1)} %copy-done.6, bf16[1040,256]{1,0:T(8,128)(2,1)} %get-tuple-element.35.sc_ref), custom_call_target="tpu_custom_call" | custom-call | tf_op jit(solution)/shard_map/state_out/pallas_call | solution.py:339
  (77 shorter events, 10.0 us)
Async XLA Ops:
  7.2 49.8 %all-gather.3.cloned.1.call-start = ((), (), s32[]{:S(2)}) async-start(), calls=%async_computation.4 | async-start | bytes 2662400 | tf_op jit(solution)/shard_map/all_gather | solution.py:363
  9.2 2.2 %copy-start = (bf16[1,128,16384]{2,1,0:T(8,128)(2,1)S(1)}, bf16[1,128,16384]{2,1,0:T(8,128)(2,1)}, u32[]{:S(2)}) copy-start(bf16[1,128,16384]{2,1,0:T(8,128)(2,1)} %cot_ref.1) | copy-start | bytes 12582916
  11.3 1.0 copy-start.2
  12.4 1.0 copy-start.3
  13.4 0.9 copy-start.7
  17.8 0.8 copy-start.27
  18.6 0.8 copy-start.29
  19.4 0.8 copy-start.30
  21.6 48.3 %copy-start.15 = (bf16[128,2688]{1,0:T(8,128)(2,1)}, bf16[128,2688]{1,0:T(8,128)(2,1)S(1)}, u32[]{:S(2)}) copy-start(bf16[128,2688]{1,0:T(8,128)(2,1)S(1)} %get-tuple-element.31.refs_0_.refs_4_.refs_8_) | copy-start | bytes 2064388
  21.6 134.2 %reduce-scatter.3.cloned.1.call-start = ((), (), s32[]{:S(2)}) async-start(), calls=%async_computation.2 | async-start | bytes 2621440 | tf_op jit(solution)/shard_map/reduce_scatter | solution.py:372
  21.6 18.4 %collective-permute-start = (bf16[128,2688]{1,0:T(8,128)(2,1)S(1)}, bf16[128,2688]{1,0:T(8,128)(2,1)S(1)}, u32[]{:S(2)}, u32[]{:S(2)}) collective-permute-start(bf16[128,2688]{1,0:T(8,128)(2,1)S(1)} %get-tuple-element.32), channel_id=1, source_target_pairs={{0,4},{4,8},{8,12},{12,0},{1,5},{5,9},{9,13},{13,1},{2,6},{6,10},{... | collective-permute-start | bytes 2064392 | tf_op jit(solution)/shard_map/ppermute | solution.py:366
  23.2 19.9 %collective-permute-start.1 = (bf16[128,2688]{1,0:T(8,128)(2,1)S(1)}, bf16[128,2688]{1,0:T(8,128)(2,1)S(1)}, u32[]{:S(2)}, u32[]{:S(2)}) collective-permute-start(bf16[128,2688]{1,0:T(8,128)(2,1)S(1)} %get-tuple-element.33), channel_id=1, source_target_pairs={{0,8},{4,12},{8,0},{12,4},{1,9},{5,13},{9,1},{13,5},{2,10},{6,14},... | collective-permute-start | bytes 2064392 | tf_op jit(solution)/shard_map/ppermute | solution.py:366
  24.3 31.4 %collective-permute-start.2 = (bf16[128,2688]{1,0:T(8,128)(2,1)S(1)}, bf16[128,2688]{1,0:T(8,128)(2,1)S(1)}, u32[]{:S(2)}, u32[]{:S(2)}) collective-permute-start(bf16[128,2688]{1,0:T(8,128)(2,1)S(1)} %get-tuple-element.34), channel_id=1, source_target_pairs={{0,12},{4,0},{8,4},{12,8},{1,13},{5,1},{9,5},{13,9},{2,14},{6,2},{... | collective-permute-start | bytes 2064392 | tf_op jit(solution)/shard_map/ppermute | solution.py:366
  40.0 0.8 copy-start.17
  43.1 0.9 copy-start.20
  55.7 0.9 copy-start.23
  56.9 1.6 copy-start.13
  58.5 1.1 copy-start.18
  59.6 1.1 copy-start.21
  60.7 1.1 copy-start.24
  61.8 38.1 %copy-start.14 = (bf16[4160,256]{1,0:T(8,128)(2,1)S(1)}, bf16[4160,256]{1,0:T(8,128)(2,1)}, u32[]{:S(2)}) copy-start(bf16[4160,256]{1,0:T(8,128)(2,1)} %all-gather.3.cloned.1.call-done) | copy-start | bytes 6389764
  69.8 0.8 copy-start.38
  72.8 82.9 %reduce-scatter.5.cloned.1.call-start = ((), (), s32[]{:S(2)}) async-start(), calls=%async_computation.3 | async-start | bytes 2621440 | tf_op jit(solution)/shard_map/reduce_scatter | solution.py:374
  72.9 15.1 %collective-permute-start.3 = (bf16[128,2048]{1,0:T(8,128)(2,1)}, bf16[128,2048]{1,0:T(8,128)(2,1)S(1)}, u32[]{:S(2)}, u32[]{:S(2)}) collective-permute-start(bf16[128,2048]{1,0:T(8,128)(2,1)} %copy-done.30), channel_id=1, source_target_pairs={{0,4},{4,8},{8,12},{12,0},{1,5},{5,9},{9,13},{13,1},{2,6},{6,10},{... | collective-permute-start | bytes 1572872 | tf_op jit(solution)/shard_map/ppermute | solution.py:366
  74.4 16.6 %collective-permute-start.4 = (bf16[128,2048]{1,0:T(8,128)(2,1)}, bf16[128,2048]{1,0:T(8,128)(2,1)S(1)}, u32[]{:S(2)}, u32[]{:S(2)}) collective-permute-start(bf16[128,2048]{1,0:T(8,128)(2,1)} %copy-done.29), channel_id=1, source_target_pairs={{0,8},{4,12},{8,0},{12,4},{1,9},{5,13},{9,1},{13,5},{2,10},{6,14},... | collective-permute-start | bytes 1572872 | tf_op jit(solution)/shard_map/ppermute | solution.py:366
  76.2 23.7 %collective-permute-start.5 = (bf16[128,2048]{1,0:T(8,128)(2,1)S(1)}, bf16[128,2048]{1,0:T(8,128)(2,1)S(1)}, u32[]{:S(2)}, u32[]{:S(2)}) collective-permute-start(bf16[128,2048]{1,0:T(8,128)(2,1)S(1)} %get-tuple-element.40), channel_id=1, source_target_pairs={{0,12},{4,0},{8,4},{12,8},{1,13},{5,1},{9,5},{13,9},{2,14},{6,2},{... | collective-permute-start | bytes 1572872 | tf_op jit(solution)/shard_map/ppermute | solution.py:366
  99.9 1.1 copy-start.16
  101.0 1.1 copy-start.19
  102.1 1.1 copy-start.22
  103.2 1.1 copy-start.25
  104.3 1.1 copy-start.28
  105.4 1.0 copy-start.39
  106.4 1.0 copy-start.41
  107.3 1.0 copy-start.43
  108.3 1.0 copy-start.45
  109.3 14.5 %copy-start.4 = (bf16[1,128,2048]{2,1,0:T(8,128)(2,1)S(1)}, bf16[1,128,2048]{2,1,0:T(8,128)(2,1)}, u32[]{:S(2)}) copy-start(bf16[1,128,2048]{2,1,0:T(8,128)(2,1)} %c_ref.1) | copy-start | bytes 1572868
  109.3 14.5 %copy-start.26 = (bf16[1,128,2048]{2,1,0:T(8,128)(2,1)S(1)}, bf16[1,128,2048]{2,1,0:T(8,128)(2,1)}, u32[]{:S(2)}) copy-start(bf16[1,128,2048]{2,1,0:T(8,128)(2,1)} %b_ref.1) | copy-start | bytes 1572868
  119.1 35.5 %collective-permute-start.6 = (f32[128,640]{1,0:T(8,128)}, f32[128,640]{1,0:T(8,128)S(1)}, u32[]{:S(2)}, u32[]{:S(2)}) collective-permute-start(f32[128,640]{1,0:T(8,128)} %copy-done.33), channel_id=1, source_target_pairs={{0,12},{4,0},{8,4},{12,8},{1,13},{5,1},{9,5},{13,9},{2,14},{6,2},{... | collective-permute-start | bytes 983048 | tf_op jit(solution)/shard_map/ppermute | solution.py:375
  120.0 34.6 %collective-permute-start.7 = (f32[128,640]{1,0:T(8,128)}, f32[128,640]{1,0:T(8,128)S(1)}, u32[]{:S(2)}, u32[]{:S(2)}) collective-permute-start(f32[128,640]{1,0:T(8,128)} %copy-done.32), channel_id=1, source_target_pairs={{0,8},{4,12},{8,0},{12,4},{1,9},{5,13},{9,1},{13,5},{2,10},{6,14},... | collective-permute-start | bytes 983048 | tf_op jit(solution)/shard_map/ppermute | solution.py:375
  122.1 32.5 %collective-permute-start.8 = (f32[128,640]{1,0:T(8,128)}, f32[128,640]{1,0:T(8,128)S(1)}, u32[]{:S(2)}, u32[]{:S(2)}) collective-permute-start(f32[128,640]{1,0:T(8,128)} %copy-done.31), channel_id=1, source_target_pairs={{0,4},{4,8},{8,12},{12,0},{1,5},{5,9},{9,13},{13,1},{2,6},{6,10},{... | collective-permute-start | bytes 983048 | tf_op jit(solution)/shard_map/ppermute | solution.py:375
  123.8 2.2 %copy-start.1 = (bf16[1,128,16384]{2,1,0:T(8,128)(2,1)S(1)}, bf16[1,128,16384]{2,1,0:T(8,128)(2,1)}, u32[]{:S(2)}) copy-start(bf16[1,128,16384]{2,1,0:T(8,128)(2,1)} %cot_ref.1) | copy-start | bytes 12582916
  126.0 2.2 %copy-start.12 = (bf16[1,128,16384]{2,1,0:T(8,128)(2,1)S(1)}, bf16[1,128,16384]{2,1,0:T(8,128)(2,1)}, u32[]{:S(2)}) copy-start(bf16[1,128,16384]{2,1,0:T(8,128)(2,1)} %x_ref.1) | copy-start | bytes 12582916
  128.2 0.9 copy-start.35
  129.1 0.9 copy-start.37
  130.0 24.6 %copy-start.8 = (f32[1,128,256]{2,1,0:T(8,128)S(1)}, f32[1,128,256]{2,1,0:T(8,128)}, u32[]{:S(2)}) copy-start(f32[1,128,256]{2,1,0:T(8,128)} %dt_ref.3) | copy-start | bytes 393220
  130.0 24.6 %copy-start.11 = (f32[256]{0:T(256)S(1)}, f32[256]{0:T(256)}, u32[]{:S(2)}) copy-start(f32[256]{0:T(256)} %param.16) | copy-start | bytes 3076
  155.8 1.0 copy-start.5
  156.8 1.0 copy-start.6
  (10 other events, 7.1 us)
Sparse Core Ops, SparseCore 0:
  21.7 35.1 all-gather.2
  73.0 33.1 reduce-scatter.2
  119.2 33.1 reduce-scatter.4

commit v2 on v1

v2 whole, which is shorter than its diff:
```python
import functools

import jax
import jax.numpy as jnp
from jax import lax
from jax.experimental import pallas as pl
from jax.experimental.pallas import tpu as pltpu
from jax.sharding import Mesh, PartitionSpec as P

F32 = jnp.float32
BF16 = jnp.bfloat16

TOK = 128
H = 256
PS = 64
N = 256
G = 8
ROW = 4
RH = H // ROW
OH = RH // ROW
OW = OH * PS
RW = RH * PS
CHS = (8, 8)
CWS = (CHS[0] * PS, CHS[1] * PS)
ATS = (0, CWS[0])
PWS = (ROW * CWS[0], ROW * CWS[1])
PACK0 = PWS[0] + 2 * N + 2 * RH
PAD = 16
TOP = 32752.0
MIB = 1024 * 1024
VMEM = 28 * MIB
SMALL = pl.CostEstimate(flops=1000, bytes_accessed=1000, transcendentals=0)


def dot(a, b):
    return lax.dot_general(a, b, (((1,), (0,)), ((), ())), preferred_element_type=F32)


def dot_nt(a, b):
    return lax.dot_general(a, b, (((1,), (1,)), ((), ())), preferred_element_type=F32)


def dot_tn(a, b):
    return lax.dot_general(a, b, (((0,), (0,)), ((), ())), preferred_element_type=F32)


def split2(a):
    hi = a.astype(BF16)
    lo = (a - hi.astype(F32)).astype(BF16)
    return hi, lo


def split3(a):
    hi = a.astype(BF16)
    rest = a - hi.astype(F32)
    mid = rest.astype(BF16)
    lo = (rest - mid.astype(F32)).astype(BF16)
    return hi, mid, lo


def iota(shape, dim):
    return lax.broadcasted_iota(jnp.int32, shape, dim)


def scale_row(held, chunk):
    first = ATS[chunk] // N
    rows = [held[q : q + 1] for q in range(first, first + CWS[chunk] // N)]
    return jnp.concatenate(rows, axis=1)


def softplus(a):
    return jnp.maximum(a, 0.0) + jnp.log1p(jnp.exp(-jnp.abs(a)))


def in_hbm(*arrays):
    return [pltpu.with_memory_space_constraint(a, pltpu.HBM) for a in arrays]


def prep_kernel(
    x_idx, y_idx, sign, adv, length, dt_hbm, rate_hbm, scale_hbm, cot_hbm, c_hbm, codes_hbm, *rest
):
    packs0, packs1 = rest[0:4], rest[4:8]
    stp, ep_ref, fp_ref, dt_ref, rate_ref, scale_ref, cot_v, c_v, codes_v, sc_ref, sems = rest[8:19]
    me = x_idx[0]
    order = (2, 1, 3, 0)
    owners = [lax.rem(y_idx[0] + ROW - j, ROW) for j in range(ROW)]
    started = []

    def start(src, dst):
        copy = pltpu.make_async_copy(src, dst, sems.at[len(started)])
        copy.start()
        started.append(copy)
        return copy

    load_dt = start(dt_hbm, dt_ref)
    load_rate = start(rate_hbm, rate_ref)
    load_scale = start(scale_hbm, scale_ref)
    loads = {}
    for k in order:
        there = lax.rem(me + k, ROW)
        at = pl.multiple_of(there * RW, RW)
        loads[k] = start(cot_hbm.at[0, :, pl.ds(at, RW)], cot_v.at[k])
    load_c = start(c_hbm.at[0], c_v)
    load_codes = start(codes_hbm, codes_v)

    load_dt.wait()
    load_rate.wait()
    step = softplus(dt_ref[0])
    tri = (iota((TOK, TOK), 0) >= iota((TOK, TOK), 1)).astype(F32).astype(BF16)
    s_hi, s_mid, s_lo = split3(step)
    total = dot(tri, s_hi) + dot(tri, s_mid) + dot(tri, s_lo)
    log_decay = -rate_ref[...] * total
    weight = (2.0 * sign[0].astype(F32) - 1.0) * adv[0] / jnp.full((TOK, H), length[0], jnp.int32).astype(F32)
    weight = jnp.where(iota((TOK, H), 0) < length[0], weight, 0.0)
    e_hi, e_lo = split2(weight * jnp.exp(log_decay))
    f_hi, f_lo = split2(step * jnp.exp(-log_decay))
    for q in range(ROW):
        cols = slice(q * RH, (q + 1) * RH)
        ep_ref[q] = jnp.concatenate([e_hi[:, cols], e_lo[:, cols]], axis=1)
        fp_ref[q] = jnp.concatenate([f_hi[:, cols], f_lo[:, cols]], axis=1)

    stores = []
    load_c.wait()
    for k in order:
        there = lax.rem(me + k, ROW)
        at = pl.multiple_of(there * 2 * N, 2 * N)
        stores.append(start(c_v.at[:, pl.ds(at, 2 * N)], packs0[k].at[:, pl.ds(PWS[0], 2 * N)]))
        stores.append(start(ep_ref.at[there], packs0[k].at[:, pl.ds(PWS[0] + 2 * N, 2 * RH)]))
    for k in order:
        loads[k].wait()
        for chunk, packs in enumerate((packs0, packs1)):
            width = CWS[chunk]
            for j in range(ROW):
                at = pl.multiple_of(owners[j] * OW + ATS[chunk], N)
                stores.append(
                    start(
                        cot_v.at[k, :, pl.ds(at, width)],
                        packs[k].at[:, pl.ds(j * width, width)],
                    )
                )
    load_codes.wait()
    stores.append(start(codes_v, stp.at[pl.ds(0, OW)]))

    load_scale.wait()
    scale = scale_ref[...].astype(F32)
    two = jnp.concatenate([scale, scale], axis=1)
    tiled = jnp.concatenate([two] * (OW // 128), axis=1)
    own = iota((OH, OW), 0) == iota((OH, OW), 1) // PS
    row = dot(jnp.ones((OH, OH), BF16), jnp.where(own, tiled, 0.0).astype(BF16))
    held = jnp.zeros((OH, N), F32)
    for q in range(OW // N):
        held = jnp.where(iota((OH, N), 0) == q, row[:, q * N : (q + 1) * N], held)
    sc_ref[...] = held.astype(BF16)
    stores.append(start(sc_ref, stp.at[pl.ds(OW, OH)]))
    for copy in stores:
        copy.wait()


def prep(x_idx, y_idx, sign, adv, length, dt, rate, scales, cot, c, codes):
    any_spec = pl.BlockSpec(memory_space=pl.ANY)
    hbm_spec = pl.BlockSpec(memory_space=pltpu.HBM)
    smem = pl.BlockSpec(memory_space=pltpu.SMEM)
    vmem = pl.BlockSpec(memory_space=pltpu.VMEM)
    outs = pl.pallas_call(
        prep_kernel,
        out_shape=[jax.ShapeDtypeStruct((TOK, PACK0), BF16)] * 4
        + [jax.ShapeDtypeStruct((TOK, PWS[1]), BF16)] * 4
        + [jax.ShapeDtypeStruct((OW + OH, N), BF16)]
        + [jax.ShapeDtypeStruct((ROW, TOK, 2 * RH), BF16)] * 2,
        in_specs=[smem] * 5 + [hbm_spec] * 6,
        out_specs=[any_spec] * 9 + [vmem] * 2,
        scratch_shapes=[
            pltpu.VMEM((1, TOK, H), F32),
            pltpu.VMEM((1, H), F32),
            pltpu.VMEM((OH, PS), BF16),
            pltpu.VMEM((ROW, TOK, RW), BF16),
            pltpu.VMEM((TOK, G * N), BF16),
            pltpu.VMEM((OW, N), BF16),
            pltpu.VMEM((OH, N), BF16),
            pltpu.SemaphoreType.DMA((64,)),
        ],
        compiler_params=pltpu.CompilerParams(vmem_limit_bytes=VMEM),
        cost_estimate=SMALL,
        name="prep",
    )(x_idx, y_idx, sign, adv, length, *in_hbm(dt, rate, scales, cot, c, codes))
    return outs[0:4], outs[4:8], outs[8], outs[9], outs[10]


def within_kernel(first, x_ref, cot_ref, b_ref, c_ref, ep_ref, fp_ref, *refs):
    gb_ref, gc_ref, q_ref, sr_ref, sel_ref = refs[-5:]
    g = pl.program_id(0) + first
    width = H // G * PS

    @pl.when(g == first)
    def _():
        for half in range(2):
            row = iota((2 * RH, width), 0)
            head = iota((2 * RH, width), 1) // PS + half * (H // G)
            hit = (row == head) | (row == head + RH)
            sel_ref[half] = jnp.where(hit, 1.0, 0.0).astype(BF16)

    parity = lax.rem(g, 2)
    sel = sel_ref[parity]
    wide = dot(jnp.concatenate([ep_ref[0], fp_ref[0]], axis=0), sel)
    dy = cot_ref[0].astype(F32) * wide[:TOK]
    xs = x_ref[0].astype(F32) * wide[TOK:]
    d_hi, d_lo = split2(dy)
    x_hi, x_lo = split2(xs)
    b, c = b_ref[0], c_ref[0]
    rows, cols = iota((TOK, TOK), 0), iota((TOK, TOK), 1)
    s_hi, s_lo = split2(jnp.where(rows >= cols, dot_nt(c, b), 0.0))
    t_hi, t_lo = split2(jnp.where(rows <= cols, dot_nt(b, c), 0.0))
    d_two = jnp.concatenate([d_hi, d_lo], axis=0)
    x_two = jnp.concatenate([x_hi, x_lo], axis=0)
    y = dot(jnp.concatenate([s_hi, s_hi], axis=1), x_two) + dot(s_lo, x_hi)
    z = dot(jnp.concatenate([t_hi, t_hi], axis=1), d_two) + dot(t_lo, d_hi)
    ds4 = dot_nt(d_two, x_two)
    ds = ds4[:TOK, :TOK] + ds4[:TOK, TOK:] + ds4[TOK:, :TOK] + ds4[TOK:, TOK:]
    ds = jnp.where(rows >= cols, ds, 0.0)
    gb_ref[0] = dot(
        jnp.concatenate(split2(ds.T), axis=1), jnp.concatenate([c, c], axis=0)
    ).astype(BF16)
    gc_ref[...] = dot(jnp.concatenate(split2(ds), axis=1), jnp.concatenate([b, b], axis=0))
    q_hi, q_lo = split2(dy * y)
    r_hi, r_lo = split2(xs * z)
    seg = dot_nt(jnp.concatenate([q_hi, q_lo, r_hi, r_lo], axis=0), sel)
    q = seg[:TOK] + seg[TOK : 2 * TOK]
    sr = seg[2 * TOK : 3 * TOK] + seg[3 * TOK :]

    @pl.when(parity == 0)
    def _():
        q_ref[0] = q
        sr_ref[0] = sr

    @pl.when(parity == 1)
    def _():
        q_ref[0] += q
        sr_ref[0] += sr


def within(first, last, x, cot, b, c, ep, fp, done):
    width = H // G * PS
    wide = pl.BlockSpec((1, TOK, width), lambda g: (0, 0, g + first))
    narrow = pl.BlockSpec((1, TOK, N), lambda g: (0, 0, g + first))
    pair = pl.BlockSpec((1, TOK, 2 * RH), lambda g: ((g + first) // 2, 0, 0))
    return pl.pallas_call(
        functools.partial(within_kernel, first),
        grid=(last - first,),
        out_shape=[
            jax.ShapeDtypeStruct((1, TOK, G * N), BF16),
            jax.ShapeDtypeStruct((TOK, G * N), F32),
            jax.ShapeDtypeStruct((ROW, TOK, 2 * RH), F32),
            jax.ShapeDtypeStruct((ROW, TOK, 2 * RH), F32),
        ],
        in_specs=[wide, wide, narrow, narrow, pair, pair]
        + [pl.BlockSpec(memory_space=pl.ANY)] * len(done),
        out_specs=[narrow, pl.BlockSpec((TOK, N), lambda g: (0, g + first)), pair, pair],
        scratch_shapes=[pltpu.VMEM((2, 2 * RH, width), BF16)],
        input_output_aliases={6 + i: i for i in range(len(done))},
        compiler_params=pltpu.CompilerParams(vmem_limit_bytes=VMEM),
        cost_estimate=SMALL,
        name=f"within{first}",
    )(*in_hbm(x, cot, b, c), ep, fp, *done)


def owner_kernel(chunk, y_idx, *refs):
    cots, cs, es = refs[0:4], refs[4:8], refs[8:12]
    codes_refs, sc_refs = refs[12:16], refs[16:20]
    olds = refs[20:24] if chunk else None
    outs = refs[24:] if chunk else refs[20:]
    own_ref, sends, rets = outs[0], outs[1:4], outs[4:8]
    me = y_idx[0]
    width = CWS[chunk]
    for r in range(ROW):
        rets[r][...] = olds[r][...] if chunk else jnp.zeros_like(rets[r])
    e = jnp.concatenate([r[...] for r in es], axis=0)
    for k in (2, 1, 3, 0):
        j = lax.rem(me + ROW - k, ROW)
        half = pl.ds(pl.multiple_of(j // 2 * N, N), N)
        cot = jnp.concatenate([r[:, k * width : (k + 1) * width] for r in cots], axis=0).astype(F32)
        c = jnp.concatenate([r[:, half] for r in cs], axis=0)
        held = sc_refs[k][...].astype(F32)
        scale = scale_row(held, chunk)
        row = iota((2 * RH, width), 0)
        head = iota((2 * RH, width), 1) // PS + j * OH + ATS[chunk] // PS
        hit = (row == head) | (row == head + RH)
        sel = jnp.where(hit, 1.0, 0.0).astype(BF16)
        sel_scaled = jnp.where(hit, jnp.broadcast_to(scale, hit.shape), 0.0).astype(BF16)
        dy = cot * dot(e, sel_scaled)
        d_hi, d_lo = split2(dy)
        codes = codes_refs[k][...]
        gs = dot_tn(c, d_hi) + dot_tn(c, d_lo)
        if k == 0:
            own_ref[...] = gs
        else:
            most = jnp.max(jnp.abs(gs), axis=0, keepdims=True)
            level = jnp.clip(jnp.ceil(jnp.log2(most) * 128.0), -14000.0, 14000.0)
            unit = TOP / jnp.exp2(level * (1.0 / 128.0))
            coded = jnp.round(gs * unit).astype(jnp.int32).astype(jnp.int16)
            sends[k - 1][:N] = coded
            sends[k - 1][N:] = jnp.broadcast_to(level.astype(jnp.int32), (PAD, width)).astype(jnp.int16)
        gc = dot(d_hi, codes) + dot(d_lo, codes)
        p_hi, p_lo = split2(dy * dot_nt(c, codes))
        q = dot_nt(p_hi, sel) + dot_nt(p_lo, sel)
        for r in range(ROW):
            rows = slice(r * TOK, (r + 1) * TOK)
            rets[r][:, half] += gc[rows]
            rets[r][:, 2 * N :] += q[rows]


def owner(chunk, y_idx, cots, packs0, states, olds):
    width = CWS[chunk]
    cot_spec = pl.BlockSpec((TOK, PWS[chunk]), lambda i: (0, 0))
    c_spec = pl.BlockSpec((TOK, 2 * N), lambda i: (0, PWS[0] // (2 * N)))
    e_spec = pl.BlockSpec((TOK, 2 * RH), lambda i: (0, (PWS[0] + 2 * N) // (2 * RH)))
    ret_spec = pl.BlockSpec((TOK, 2 * N + 2 * RH), lambda i: (0, 0))
    ret_shape = jax.ShapeDtypeStruct((TOK, 2 * N + 2 * RH), F32)
    send_spec = pl.BlockSpec((N + PAD, width), lambda i: (0, 0))
    outs = pl.pallas_call(
        functools.partial(owner_kernel, chunk),
        grid=(1,),
        out_shape=[jax.ShapeDtypeStruct((N, width), F32)]
        + [jax.ShapeDtypeStruct((N + PAD, width), jnp.int16)] * 3
        + [ret_shape] * 4,
        in_specs=[pl.BlockSpec(memory_space=pltpu.SMEM)]
        + [cot_spec] * 4
        + [c_spec] * 4
        + [e_spec] * 4
        + [pl.BlockSpec((width, N), lambda i: (ATS[chunk] // width, 0))] * 4
        + [pl.BlockSpec((OH, N), lambda i: (OW // OH, 0))] * 4
        + [ret_spec] * (4 if chunk else 0),
        out_specs=[pl.BlockSpec((N, width), lambda i: (0, 0))] + [send_spec] * 3 + [ret_spec] * 4,
        compiler_params=pltpu.CompilerParams(vmem_limit_bytes=VMEM),
        cost_estimate=SMALL,
        name=f"owner{chunk}",
    )(y_idx, *cots, *packs0, *packs0, *states, *states, *(olds if chunk else ()))
    return outs[0], list(outs[1:4]), list(outs[4:8])


def tokens_kernel(x_idx, dt_ref, rate_ref, gc_ref, q_ref, sr_ref, r0, r1, r2, r3, out_gc, out_dt):
    me = x_idx[0]
    lane = iota((TOK, H), 1) // RH
    q = jnp.zeros((TOK, H), F32)
    for k, ret in enumerate((r0, r1, r2, r3)):
        there = lax.rem(me + k, ROW)
        cols = pl.ds(pl.multiple_of(there * 2 * N, 2 * N), 2 * N)
        out_gc[0, :, cols] = (gc_ref[:, cols] + ret[:, : 2 * N]).astype(BF16)
        held = ret[:, 2 * N :]
        q = jnp.where(lane == there, jnp.concatenate([held, held], axis=1), q)
    sr = jnp.zeros((TOK, H), F32)
    for b in range(ROW):
        q = q + jnp.where(lane == b, jnp.concatenate([q_ref[b]] * 2, axis=1), 0.0)
        sr = sr + jnp.where(lane == b, jnp.concatenate([sr_ref[b]] * 2, axis=1), 0.0)
    dt = dt_ref[0]
    step = softplus(dt)
    tri = (iota((TOK, TOK), 0) <= iota((TOK, TOK), 1)).astype(F32).astype(BF16)
    a_hi, a_mid, a_lo = split3(q - sr)
    tail = dot(tri, a_hi) + dot(tri, a_mid) + dot(tri, a_lo)
    d_step = sr / step - rate_ref[...] * tail
    out_dt[0] = d_step / (1.0 + jnp.exp(-dt))


def tokens(x_idx, dt, rate, gc, q, sr, rets):
    smem = pl.BlockSpec(memory_space=pltpu.SMEM)
    vmem = pl.BlockSpec(memory_space=pltpu.VMEM)
    return pl.pallas_call(
        tokens_kernel,
        out_shape=[
            jax.ShapeDtypeStruct((1, TOK, G * N), BF16),
            jax.ShapeDtypeStruct((1, TOK, H), F32),
        ],
        in_specs=[smem] + [vmem] * 9,
        out_specs=[vmem] * 2,
        compiler_params=pltpu.CompilerParams(vmem_limit_bytes=VMEM),
        cost_estimate=SMALL,
        name="tokens",
    )(x_idx, dt, rate, gc, q, sr, *rets)


def state_kernel(*refs):
    sc_ref, out_ref = refs[8:10]
    held = sc_ref[...].astype(F32)
    for chunk in range(2):
        scale = scale_row(held, chunk)
        total = refs[4 * chunk][...]
        for ref in refs[4 * chunk + 1 : 4 * chunk + 4]:
            level = ref[N:].astype(jnp.int32).astype(F32)[:1]
            unit = jnp.exp2(level * (1.0 / 128.0)) * (1.0 / TOP)
            total = total + ref[:N].astype(jnp.int32).astype(F32) * unit
        out_ref[pl.ds(ATS[chunk], CWS[chunk]), :] = (total / scale).T


def state_out(own0, got0, own1, got1, stp):
    blocks = []
    for width in CWS:
        blocks += [pl.BlockSpec((N, width), lambda i: (0, 0))]
        blocks += [pl.BlockSpec((N + PAD, width), lambda i: (0, 0))] * 3
    return pl.pallas_call(
        state_kernel,
        grid=(1,),
        out_shape=jax.ShapeDtypeStruct((OW, N), F32),
        in_specs=blocks + [pl.BlockSpec((OH, N), lambda i: (OW // OH, 0))],
        out_specs=pl.BlockSpec((OW, N), lambda i: (0, 0)),
        compiler_params=pltpu.CompilerParams(vmem_limit_bytes=VMEM),
        cost_estimate=SMALL,
        name="state_out",
    )(own0, *got0, own1, *got1, stp)


def shift(k):
    return [(i, (i + k) % ROW) for i in range(ROW)]


def per_device(
    inputs, cotangent, b_proj, c_proj, dt_raw, decay_rate, state_codes, state_scales, sign, adv, lengths
):
    x_idx = lax.axis_index("rx").astype(jnp.int32)[None]
    y_idx = lax.axis_index("ry").astype(jnp.int32)[None]
    rate = decay_rate[None]
    packs0, packs1, stp, ep, fp = prep(
        x_idx, y_idx, sign, adv, lengths, dt_raw, rate, state_scales, cotangent, c_proj,
        state_codes.reshape(OW, N),
    )
    barrier = lax.optimization_barrier
    args = (inputs, cotangent, b_proj, c_proj, ep, fp)

    got0 = {k: lax.ppermute(packs0[k], "rx", shift(k)) for k in (2, 1, 3)}
    got0[0] = packs0[0]
    got0 = [got0[k] for k in range(ROW)]
    states = [stp, lax.ppermute(stp, "ry", shift(1)), None, lax.ppermute(stp, "ry", shift(3))]
    first = within(0, 4, *args, ())
    gc_part, state, states[1], states[3] = barrier((first[1], stp, states[1], states[3]))
    states[2] = lax.ppermute(state, "ry", shift(2))
    second = within(4, 6, *args, (first[0], gc_part, *first[2:]))
    gc_part, *send1 = barrier((second[1], *packs1[1:]))
    got1 = [packs1[0]] + [lax.ppermute(send1[k - 1], "rx", shift(k)) for k in (1, 2, 3)]
    gc_part, got0[0] = barrier((gc_part, got0[0]))
    own0, send0, rets0 = owner(0, y_idx, got0, got0, states, None)
    red0 = [None, lax.ppermute(send0[1], "ry", shift(-2)), lax.ppermute(send0[2], "ry", shift(-3))]
    gc_part, rets0[0] = barrier((gc_part, rets0[0]))
    grad_b, gc_part, q, sr = within(6, 8, *args, (second[0], gc_part, *second[2:]))
    gc_part, rets0[0], got1[0] = barrier((gc_part, rets0[0], got1[0]))
    last, *got1 = barrier((send0[0], *got1))
    red0[0] = lax.ppermute(last, "ry", shift(-1))
    red0[1], red0[2], got1[0] = barrier((red0[1], red0[2], got1[0]))
    own1, send1, rets1 = owner(1, y_idx, got1, got0, states, rets0)
    red0[0], a = barrier((red0[0], send1[0]))
    b, c = send1[1:]
    back = [rets1[0]] + [lax.ppermute(rets1[k], "rx", shift(-k)) for k in (1, 2, 3)]
    red1 = [lax.ppermute(send, "ry", shift(-k)) for k, send in ((1, a), (2, b), (3, c))]
    grad_c, grad_dt = tokens(x_idx, dt_raw, rate, gc_part, q, sr, back)
    grad_state = state_out(own0, red0, own1, red1, stp)
    return grad_state.reshape(OH, PS, N), grad_b, grad_c, grad_dt


def solution(mesh):
    prompts = mesh.shape["prompt"]
    mesh3 = Mesh(mesh.devices.reshape(prompts, ROW, ROW), ("prompt", "rx", "ry"))
    split = ("prompt", "rx", "ry")
    three = P(split, None, None)
    return jax.shard_map(
        per_device,
        mesh=mesh3,
        in_specs=(three,) * 5 + (P(), three, P(split, None)) + (P(split),) * 3,
        out_specs=(three,) * 4,
        check_vma=False,
    )
```

time: 169 us -> 99.2 us (0.59); the launches traced: 166 us -> 99.1 us
  local copies, waits for them, and re-layouts: 40.5 us -> 0.01 us
  waiting for transfers between devices: 50.2 us -> 19.6 us
  starting transfers between devices: 14.4 us -> 30.3 us
  between operations: 15.8 us -> 2.66 us
    unnamed x92 -> x4, local copies, waits for them, and re-layouts: 40.5 us -> 0.01 us
    ppermute x6 -> x15, waiting for transfers between devices: 49.8 us -> 19.6 us  [the longest x3 15.2 us: per_device(): lax.ppermute(send, 'ry', shift(-k))]
    ppermute x6 -> x15, starting transfers between devices: 9.62 us -> 26.4 us  [the longest x3 4.83 us: per_device(): got0 = {k: lax.ppermute(packs0[k], 'rx', shift(k)) for k in (2, 1, 3)}]
    pallas_call x1, Pallas kernels: 2.1 us -> 4.11 us  [prep(): pl.pallas_call(prep_kernel, out_shape=[jax.ShapeDtypeStruct((TOK, PACK0),...]
    pallas_call x3 -> x5, Pallas kernels: 40.1 us -> 39.7 us  [the longest x3 28.9 us: within(): pl.pallas_call(functools.partial(within_kernel, first), grid=(last - firs...]
  transfers between devices with their start and end apart: 12 -> 18, of which waited for: 7 -> 5; matrix products, arithmetic and copies ran while one was open for 0% -> 0% of each run, Pallas kernels for 20% -> 42%
where the time goes in v2:
time: 99.2 us; the launch traced here: 99.1 us
  Pallas kernels  46.5 us (47%)
  starting transfers between devices  30.3 us (31%)
  waiting for transfers between devices  19.6 us (20%)
  between operations  2.66 us (3%)
    pallas_call x3, Pallas kernels, within(): pl.pallas_call(functools.partial(within_kernel, first), grid=(last - firs...  28.9 us
    ppermute x3, waiting for transfers between devices, per_device(): lax.ppermute(send, 'ry', shift(-k))  15.2 us
    pallas_call x2, Pallas kernels, owner(): pl.pallas_call(functools.partial(owner_kernel, chunk), grid=(1,), out_sha...  10.8 us
    ppermute x3, starting transfers between devices, per_device(): got0 = {k: lax.ppermute(packs0[k], 'rx', shift(k)) for k in (2, 1, 3)}  4.83 us
    ppermute x3, starting transfers between devices, per_device(): lax.ppermute(send1[k - 1], 'rx', shift(k))  4.51 us
    ppermute x3, starting transfers between devices, per_device(): lax.ppermute(send, 'ry', shift(-k))  4.34 us
    pallas_call x1, Pallas kernels, prep(): pl.pallas_call(prep_kernel, out_shape=[jax.ShapeDtypeStruct((TOK, PACK0),...  4.11 us
    ppermute x3, starting transfers between devices, per_device(): lax.ppermute(rets1[k], 'rx', shift(-k))  3.9 us
  transfers between devices with their start and end apart: 18, of which 5 were waited for; matrix products, arithmetic and copies ran while one was open for 0% of the time, Pallas kernels for 42%

profile of v2, /device:TPU:130, one launch (start us, length us, event | category | flops | bytes accessed | tf_op | source)
XLA Modules:
  0.0 99.1 jit_solution(3359624749932521134)
XLA Ops:
  2.6 4.1 %prep.1 = (bf16[128,2688]{1,0:T(8,128)(2,1)S(1)}, bf16[128,2688]{1,0:T(8,128)(2,1)S(1)}, bf16[128,2688]{1,0:T(8,128)(2,1)S(1)}, bf16[128,2688]{1,0:T(8,128)(2,1)...) custom-call(s32[1]{0:T(128)} %bitcast.1.x_idx, ...), custom_call_target="tpu_custom_call" | custom-call | flops 1000 | bytes 1000 | tf_op jit(solution)/shard_map/prep/pallas_call | solution.py:164
  6.7 1.6 %collective-permute-start.2 = (bf16[128,2688]{1,0:T(8,128)(2,1)S(1)}, bf16[128,2688]{1,0:T(8,128)(2,1)S(1)}, u32[]{:S(2)}, u32[]{:S(2)}) collective-permute-start(bf16[128,2688]{1,0:T(8,128)(2,1)S(1)} %get-tuple-element.85), channel_id=1, source_target_pairs={{0,4},{4,8},{8,12},{12,0},{1,5},{5,9},{9,13},{13,1},{2,6},{6,10},{... | collective-permute-start | bytes 2064392 | tf_op jit(solution)/shard_map/ppermute | solution.py:427
  8.3 1.1 %collective-permute-start.3 = (bf16[128,2688]{1,0:T(8,128)(2,1)S(1)}, bf16[128,2688]{1,0:T(8,128)(2,1)S(1)}, u32[]{:S(2)}, u32[]{:S(2)}) collective-permute-start(bf16[128,2688]{1,0:T(8,128)(2,1)S(1)} %get-tuple-element.86), channel_id=1, source_target_pairs={{0,8},{4,12},{8,0},{12,4},{1,9},{5,13},{9,1},{13,5},{2,10},{6,14},... | collective-permute-start | bytes 2064392 | tf_op jit(solution)/shard_map/ppermute | solution.py:427
  9.4 3.0 %collective-permute-start.1 = (bf16[1040,256]{1,0:T(8,128)(2,1)S(1)}, bf16[1040,256]{1,0:T(8,128)(2,1)S(1)}, u32[]{:S(2)}, u32[]{:S(2)}) collective-permute-start(bf16[1040,256]{1,0:T(8,128)(2,1)S(1)} %get-tuple-element.89.refs_12_.refs_16_.refs_8_), channel_id=1, source_target_pairs={{0,3},{1,0},{2,1},{3,2},{4,7},{5,4},{6,5},{7,6},{8,11},{9,8},{10,9... | collective-permute-start | bytes 1597448 | tf_op jit(solution)/shard_map/ppermute | solution.py:430
  12.4 0.0 collective-permute-start
  12.4 2.2 %collective-permute-start.4 = (bf16[128,2688]{1,0:T(8,128)(2,1)S(1)}, bf16[128,2688]{1,0:T(8,128)(2,1)S(1)}, u32[]{:S(2)}, u32[]{:S(2)}) collective-permute-start(bf16[128,2688]{1,0:T(8,128)(2,1)S(1)} %get-tuple-element.87), channel_id=1, source_target_pairs={{0,12},{4,0},{8,4},{12,8},{1,13},{5,1},{9,5},{13,9},{2,14},{6,2},{... | collective-permute-start | bytes 2064392 | tf_op jit(solution)/shard_map/ppermute | solution.py:427
  14.5 13.5 %within0.1 = (bf16[1,128,2048]{2,1,0:T(8,128)(2,1)}, f32[128,2048]{1,0:T(8,128)S(1)}, f32[4,128,128]{2,1,0:T(8,128)S(1)}, f32[4,128,128]{2,1,0:T(8,128)S(1)}) custom-call(bf16[1,128,16384]{2,1,0:T(8,128)(2,1)} %x_ref.5, bf16[1,128,16384]{2,1,0:T(8,128)(2,1)} %cot_ref.5, bf16[1,128,2048]{2,1,0:T(8,128)(2,1)} %b_ref.5, bf16[1,128,2048]{2,1,0:T(8,128)(2,1)} %c_ref.5, ...), custom_call_target="tpu_custom_call" | custom-call | flops 1000 | bytes 1000 | tf_op jit(solution)/shard_map/within0/pallas_call | solution.py:246
  28.0 0.0 collective-permute-done.1.refs_15_.refs_19_
  28.0 0.0 collective-permute-done.refs_13_.refs_17_
  28.0 2.3 %collective-permute-start.5 = (bf16[1040,256]{1,0:T(8,128)(2,1)S(1)}, bf16[1040,256]{1,0:T(8,128)(2,1)S(1)}, u32[]{:S(2)}, u32[]{:S(2)}) collective-permute-start(bf16[1040,256]{1,0:T(8,128)(2,1)S(1)} %get-tuple-element.89.refs_12_.refs_16_.refs_8_), channel_id=1, source_target_pairs={{0,2},{1,3},{2,0},{3,1},{4,6},{5,7},{6,4},{7,5},{8,10},{9,11},{10,... | collective-permute-start | bytes 1597448 | tf_op jit(solution)/shard_map/ppermute | solution.py:433
  30.3 7.7 %within4.1 = (bf16[1,128,2048]{2,1,0:T(8,128)(2,1)}, f32[128,2048]{1,0:T(8,128)S(1)}, f32[4,128,128]{2,1,0:T(8,128)S(1)}, f32[4,128,128]{2,1,0:T(8,128)S(1)}) custom-call(bf16[1,128,16384]{2,1,0:T(8,128)(2,1)} %x_ref.5, bf16[1,128,16384]{2,1,0:T(8,128)(2,1)} %cot_ref.5, ...), custom_call_target="tpu_custom_call", output_to_operand_aliasing={{0}: (6, {}), {1}: (7, {}), {2}: (8, {}), {3}: (9, {})} | custom-call | flops 1000 | bytes 1000 | tf_op jit(solution)/shard_map/within4/pallas_call | solution.py:246
  38.0 0.0 collective-permute-start.6
  38.0 0.0 collective-permute-done.2.refs_1_.refs_5_.refs_9_
  38.0 3.5 %collective-permute-start.7 = (bf16[128,2048]{1,0:T(8,128)(2,1)S(1)}, bf16[128,2048]{1,0:T(8,128)(2,1)S(1)}, u32[]{:S(2)}, u32[]{:S(2)}) collective-permute-start(bf16[128,2048]{1,0:T(8,128)(2,1)S(1)} %get-tuple-element.104), channel_id=1, source_target_pairs={{0,8},{4,12},{8,0},{12,4},{1,9},{5,13},{9,1},{13,5},{2,10},{6,14},... | collective-permute-start | bytes 1572872 | tf_op jit(solution)/shard_map/ppermute | solution.py:436
  41.6 0.0 collective-permute-done.3.refs_2_.refs_6_.refs_10_
  41.6 1.0 %collective-permute-start.8 = (bf16[128,2048]{1,0:T(8,128)(2,1)S(1)}, bf16[128,2048]{1,0:T(8,128)(2,1)S(1)}, u32[]{:S(2)}, u32[]{:S(2)}) collective-permute-start(bf16[128,2048]{1,0:T(8,128)(2,1)S(1)} %get-tuple-element.105), channel_id=1, source_target_pairs={{0,12},{4,0},{8,4},{12,8},{1,13},{5,1},{9,5},{13,9},{2,14},{6,2},{... | collective-permute-start | bytes 1572872 | tf_op jit(solution)/shard_map/ppermute | solution.py:436
  42.6 0.0 collective-permute-done.4.refs_3_.refs_7_.refs_11_
  42.6 0.0 collective-permute-done.5.refs_14_.refs_18_
  42.6 5.4 %owner0.1 = (f32[256,512]{1,0:T(8,128)S(1)}, s16[272,512]{1,0:T(8,128)(2,1)S(1)}, s16[272,512]{1,0:T(8,128)(2,1)S(1)}, s16[272,512]{1,0:T(8,128)(2,1)S(1)}, f32[...) custom-call(s32[1]{0:T(128)} %bitcast.y_idx, ...), custom_call_target="tpu_custom_call" | custom-call | flops 1000 | bytes 1000 | tf_op jit(solution)/shard_map/owner0/pallas_call | solution.py:319
  48.0 3.7 %collective-permute-start.10 = (s16[272,512]{1,0:T(8,128)(2,1)S(1)}, s16[272,512]{1,0:T(8,128)(2,1)S(1)}, u32[]{:S(2)}, u32[]{:S(2)}) collective-permute-start(s16[272,512]{1,0:T(8,128)(2,1)S(1)} %get-tuple-element.107), channel_id=1, source_target_pairs={{0,2},{1,3},{2,0},{3,1},{4,6},{5,7},{6,4},{7,5},{8,10},{9,11},{10,... | collective-permute-start | bytes 835592 | tf_op jit(solution)/shard_map/ppermute | solution.py:439
  51.7 0.7 collective-permute-start.11
  52.3 7.7 %within6.1 = (bf16[1,128,2048]{2,1,0:T(8,128)(2,1)}, f32[128,2048]{1,0:T(8,128)S(1)}, f32[4,128,128]{2,1,0:T(8,128)S(1)}, f32[4,128,128]{2,1,0:T(8,128)S(1)}) custom-call(bf16[1,128,16384]{2,1,0:T(8,128)(2,1)} %x_ref.5, bf16[1,128,16384]{2,1,0:T(8,128)(2,1)} %cot_ref.5, ...), custom_call_target="tpu_custom_call", output_to_operand_aliasing={{0}: (6, {}), {1}: (7, {}), {2}: (8, {}), {3}: (9, {})} | custom-call | flops 1000 | bytes 1000 | tf_op jit(solution)/shard_map/within6/pallas_call | solution.py:246
  60.1 0.0 collective-permute-done.6.refs_1_
  60.1 0.0 collective-permute-done.7.refs_2_
  60.1 3.8 %collective-permute-done.8.refs_3_ = bf16[128,2048]{1,0:T(8,128)(2,1)S(1)} collective-permute-done((bf16[128,2048]{1,0:T(8,128)(2,1)S(1)}, bf16[128,2048]{1,0:T(8,128)(2,1)S(1)}, u32[]{:S(2)}, u32[]{:S(2)}) %collective-permute-start.8) | collective-permute-done | bytes 524320 | tf_op jit(solution)/shard_map/ppermute | solution.py:436
  63.9 3.0 %collective-permute-start.9 = (s16[272,512]{1,0:T(8,128)(2,1)S(1)}, s16[272,512]{1,0:T(8,128)(2,1)S(1)}, u32[]{:S(2)}, u32[]{:S(2)}) collective-permute-start(s16[272,512]{1,0:T(8,128)(2,1)S(1)} %get-tuple-element.106), channel_id=1, source_target_pairs={{0,3},{1,0},{2,1},{3,2},{4,7},{5,4},{6,5},{7,6},{8,11},{9,8},{10,9... | collective-permute-start | bytes 835592 | tf_op jit(solution)/shard_map/ppermute | solution.py:444
  66.9 0.0 collective-permute-done.10.refs_2_
  66.9 0.0 collective-permute-done.11.refs_3_
  66.9 5.4 %owner1.1 = (f32[256,512]{1,0:T(8,128)S(1)}, s16[272,512]{1,0:T(8,128)(2,1)S(1)}, s16[272,512]{1,0:T(8,128)(2,1)S(1)}, s16[272,512]{1,0:T(8,128)(2,1)S(1)}, f32[...) custom-call(s32[1]{0:T(128)} %bitcast.y_idx, ...), custom_call_target="tpu_custom_call" | custom-call | flops 1000 | bytes 1000 | tf_op jit(solution)/shard_map/owner1/pallas_call | solution.py:319
  72.3 0.0 copy-start
  72.3 0.0 copy-start.1
  72.3 0.6 collective-permute-done.9.refs_1_
  72.9 3.7 %collective-permute-start.12 = (s16[272,512]{1,0:T(8,128)(2,1)S(1)}, s16[272,512]{1,0:T(8,128)(2,1)S(1)}, u32[]{:S(2)}, u32[]{:S(2)}) collective-permute-start(s16[272,512]{1,0:T(8,128)(2,1)S(1)} %get-tuple-element.123), channel_id=1, source_target_pairs={{0,3},{1,0},{2,1},{3,2},{4,7},{5,4},{6,5},{7,6},{8,11},{9,8},{10,9... | collective-permute-start | bytes 835592 | tf_op jit(solution)/shard_map/ppermute | solution.py:450
  76.6 0.0 collective-permute-start.15
  76.6 1.3 %collective-permute-start.16 = (f32[128,640]{1,0:T(8,128)S(1)}, f32[128,640]{1,0:T(8,128)S(1)}, u32[]{:S(2)}, u32[]{:S(2)}) collective-permute-start(f32[128,640]{1,0:T(8,128)S(1)} %get-tuple-element.132), channel_id=1, source_target_pairs={{0,8},{4,12},{8,0},{12,4},{1,9},{5,13},{9,1},{13,5},{2,10},{6,14},... | collective-permute-start | bytes 983048 | tf_op jit(solution)/shard_map/ppermute | solution.py:449
  77.8 2.6 %collective-permute-start.17 = (f32[128,640]{1,0:T(8,128)S(1)}, f32[128,640]{1,0:T(8,128)S(1)}, u32[]{:S(2)}, u32[]{:S(2)}) collective-permute-start(f32[128,640]{1,0:T(8,128)S(1)} %get-tuple-element.133), channel_id=1, source_target_pairs={{0,4},{4,8},{8,12},{12,0},{1,5},{5,9},{9,13},{13,1},{2,6},{6,10},{... | collective-permute-start | bytes 983048 | tf_op jit(solution)/shard_map/ppermute | solution.py:449
  80.5 0.6 collective-permute-start.13
  81.1 6.6 %collective-permute-done.12.refs_5_ = s16[272,512]{1,0:T(8,128)(2,1)S(1)} collective-permute-done((s16[272,512]{1,0:T(8,128)(2,1)S(1)}, s16[272,512]{1,0:T(8,128)(2,1)S(1)}, u32[]{:S(2)}, u32[]{:S(2)}) %collective-permute-start.12) | collective-permute-done | bytes 278560 | tf_op jit(solution)/shard_map/ppermute | solution.py:450
  87.7 0.0 collective-permute-start.14
  87.7 0.9 collective-permute-done.13.refs_6_
  88.6 7.7 %collective-permute-done.14.refs_7_ = s16[272,512]{1,0:T(8,128)(2,1)S(1)} collective-permute-done((s16[272,512]{1,0:T(8,128)(2,1)S(1)}, s16[272,512]{1,0:T(8,128)(2,1)S(1)}, u32[]{:S(2)}, u32[]{:S(2)}) %collective-permute-start.14) | collective-permute-done | bytes 278560 | tf_op jit(solution)/shard_map/ppermute | solution.py:450
  96.3 1.5 %state_out.1 = f32[1024,256]{1,0:T(8,128)} custom-call(f32[256,512]{1,0:T(8,128)S(1)} %get-tuple-element.91.refs_0_, s16[272,512]{1,0:T(8,128)(2,1)S(1)} %collective-permute-done.9.refs_1_, s16[272,512]{1,0:T(8,128)(2,1)S(1)} %collective-permute-done.10.refs_2_, s16[272,512]{1,0:T(8,128)(2,1)S(1)} %collective-permute-done.11.refs_3_, ...), custom_call_target="tpu_custom_call" | custom-call | flops 1000 | bytes 1000 | tf_op jit(solution)/shard_map/state_out/pallas_call | solution.py:398
  97.8 0.0 collective-permute-done.15.r1
  97.8 0.0 collective-permute-done.16.r2
  97.8 0.0 collective-permute-done.17.r3
  97.8 0.0 copy-done
  97.8 0.0 copy-done.1
  97.8 1.2 %tokens.1 = (bf16[1,128,2048]{2,1,0:T(8,128)(2,1)}, f32[1,128,256]{2,1,0:T(8,128)}) custom-call(s32[1]{0:T(128)} %bitcast.1.x_idx, f32[1,128,256]{2,1,0:T(8,128)S(1)} %copy-done, f32[1,256]{1,0:T(1,128)S(1)} %bitcast.6, f32[128,2048]{1,0:T(8,128)S(1)} %get-tuple-element.127.gc_ref, f32[4,128,128]{2,1,0:T(8,128)S(1)} %get-tuple-element.128.q_ref, ...), custom_call_target="tpu_custom_call" | custom-call | flops 1000 | bytes 1000 | tf_op jit(solution)/shard_map/tokens/pallas_call | solution.py:366
Async XLA Ops:
  6.7 31.4 %collective-permute-start.2 = (bf16[128,2688]{1,0:T(8,128)(2,1)S(1)}, bf16[128,2688]{1,0:T(8,128)(2,1)S(1)}, u32[]{:S(2)}, u32[]{:S(2)}) collective-permute-start(bf16[128,2688]{1,0:T(8,128)(2,1)S(1)} %get-tuple-element.85), channel_id=1, source_target_pairs={{0,4},{4,8},{8,12},{12,0},{1,5},{5,9},{9,13},{13,1},{2,6},{6,10},{... | collective-permute-start | bytes 2064392 | tf_op jit(solution)/shard_map/ppermute | solution.py:427
  8.3 33.3 %collective-permute-start.3 = (bf16[128,2688]{1,0:T(8,128)(2,1)S(1)}, bf16[128,2688]{1,0:T(8,128)(2,1)S(1)}, u32[]{:S(2)}, u32[]{:S(2)}) collective-permute-start(bf16[128,2688]{1,0:T(8,128)(2,1)S(1)} %get-tuple-element.86), channel_id=1, source_target_pairs={{0,8},{4,12},{8,0},{12,4},{1,9},{5,13},{9,1},{13,5},{2,10},{6,14},... | collective-permute-start | bytes 2064392 | tf_op jit(solution)/shard_map/ppermute | solution.py:427
  9.4 18.7 %collective-permute-start.1 = (bf16[1040,256]{1,0:T(8,128)(2,1)S(1)}, bf16[1040,256]{1,0:T(8,128)(2,1)S(1)}, u32[]{:S(2)}, u32[]{:S(2)}) collective-permute-start(bf16[1040,256]{1,0:T(8,128)(2,1)S(1)} %get-tuple-element.89.refs_12_.refs_16_.refs_8_), channel_id=1, source_target_pairs={{0,3},{1,0},{2,1},{3,2},{4,7},{5,4},{6,5},{7,6},{8,11},{9,8},{10,9... | collective-permute-start | bytes 1597448 | tf_op jit(solution)/shard_map/ppermute | solution.py:430
  12.4 15.6 %collective-permute-start = (bf16[1040,256]{1,0:T(8,128)(2,1)S(1)}, bf16[1040,256]{1,0:T(8,128)(2,1)S(1)}, u32[]{:S(2)}, u32[]{:S(2)}) collective-permute-start(bf16[1040,256]{1,0:T(8,128)(2,1)S(1)} %get-tuple-element.89.refs_12_.refs_16_.refs_8_), channel_id=1, source_target_pairs={{0,1},{1,2},{2,3},{3,0},{4,5},{5,6},{6,7},{7,4},{8,9},{9,10},{10,1... | collective-permute-start | bytes 1597448 | tf_op jit(solution)/shard_map/ppermute | solution.py:430
  12.4 30.2 %collective-permute-start.4 = (bf16[128,2688]{1,0:T(8,128)(2,1)S(1)}, bf16[128,2688]{1,0:T(8,128)(2,1)S(1)}, u32[]{:S(2)}, u32[]{:S(2)}) collective-permute-start(bf16[128,2688]{1,0:T(8,128)(2,1)S(1)} %get-tuple-element.87), channel_id=1, source_target_pairs={{0,12},{4,0},{8,4},{12,8},{1,13},{5,1},{9,5},{13,9},{2,14},{6,2},{... | collective-permute-start | bytes 2064392 | tf_op jit(solution)/shard_map/ppermute | solution.py:427
  28.0 14.5 %collective-permute-start.5 = (bf16[1040,256]{1,0:T(8,128)(2,1)S(1)}, bf16[1040,256]{1,0:T(8,128)(2,1)S(1)}, u32[]{:S(2)}, u32[]{:S(2)}) collective-permute-start(bf16[1040,256]{1,0:T(8,128)(2,1)S(1)} %get-tuple-element.89.refs_12_.refs_16_.refs_8_), channel_id=1, source_target_pairs={{0,2},{1,3},{2,0},{3,1},{4,6},{5,7},{6,4},{7,5},{8,10},{9,11},{10,... | collective-permute-start | bytes 1597448 | tf_op jit(solution)/shard_map/ppermute | solution.py:433
  38.0 22.0 %collective-permute-start.6 = (bf16[128,2048]{1,0:T(8,128)(2,1)S(1)}, bf16[128,2048]{1,0:T(8,128)(2,1)S(1)}, u32[]{:S(2)}, u32[]{:S(2)}) collective-permute-start(bf16[128,2048]{1,0:T(8,128)(2,1)S(1)} %get-tuple-element.103), channel_id=1, source_target_pairs={{0,4},{4,8},{8,12},{12,0},{1,5},{5,9},{9,13},{13,1},{2,6},{6,10},{... | collective-permute-start | bytes 1572872 | tf_op jit(solution)/shard_map/ppermute | solution.py:436
  38.0 22.0 %collective-permute-start.7 = (bf16[128,2048]{1,0:T(8,128)(2,1)S(1)}, bf16[128,2048]{1,0:T(8,128)(2,1)S(1)}, u32[]{:S(2)}, u32[]{:S(2)}) collective-permute-start(bf16[128,2048]{1,0:T(8,128)(2,1)S(1)} %get-tuple-element.104), channel_id=1, source_target_pairs={{0,8},{4,12},{8,0},{12,4},{1,9},{5,13},{9,1},{13,5},{2,10},{6,14},... | collective-permute-start | bytes 1572872 | tf_op jit(solution)/shard_map/ppermute | solution.py:436
  41.6 22.3 %collective-permute-start.8 = (bf16[128,2048]{1,0:T(8,128)(2,1)S(1)}, bf16[128,2048]{1,0:T(8,128)(2,1)S(1)}, u32[]{:S(2)}, u32[]{:S(2)}) collective-permute-start(bf16[128,2048]{1,0:T(8,128)(2,1)S(1)} %get-tuple-element.105), channel_id=1, source_target_pairs={{0,12},{4,0},{8,4},{12,8},{1,13},{5,1},{9,5},{13,9},{2,14},{6,2},{... | collective-permute-start | bytes 1572872 | tf_op jit(solution)/shard_map/ppermute | solution.py:436
  48.0 18.9 %collective-permute-start.10 = (s16[272,512]{1,0:T(8,128)(2,1)S(1)}, s16[272,512]{1,0:T(8,128)(2,1)S(1)}, u32[]{:S(2)}, u32[]{:S(2)}) collective-permute-start(s16[272,512]{1,0:T(8,128)(2,1)S(1)} %get-tuple-element.107), channel_id=1, source_target_pairs={{0,2},{1,3},{2,0},{3,1},{4,6},{5,7},{6,4},{7,5},{8,10},{9,11},{10,... | collective-permute-start | bytes 835592 | tf_op jit(solution)/shard_map/ppermute | solution.py:439
  51.7 15.2 %collective-permute-start.11 = (s16[272,512]{1,0:T(8,128)(2,1)S(1)}, s16[272,512]{1,0:T(8,128)(2,1)S(1)}, u32[]{:S(2)}, u32[]{:S(2)}) collective-permute-start(s16[272,512]{1,0:T(8,128)(2,1)S(1)} %get-tuple-element.108), channel_id=1, source_target_pairs={{0,1},{1,2},{2,3},{3,0},{4,5},{5,6},{6,7},{7,4},{8,9},{9,10},{10,1... | collective-permute-start | bytes 835592 | tf_op jit(solution)/shard_map/ppermute | solution.py:439
  63.9 9.0 %collective-permute-start.9 = (s16[272,512]{1,0:T(8,128)(2,1)S(1)}, s16[272,512]{1,0:T(8,128)(2,1)S(1)}, u32[]{:S(2)}, u32[]{:S(2)}) collective-permute-start(s16[272,512]{1,0:T(8,128)(2,1)S(1)} %get-tuple-element.106), channel_id=1, source_target_pairs={{0,3},{1,0},{2,1},{3,2},{4,7},{5,4},{6,5},{7,6},{8,11},{9,8},{10,9... | collective-permute-start | bytes 835592 | tf_op jit(solution)/shard_map/ppermute | solution.py:444
  72.3 25.5 %copy-start = (f32[1,128,256]{2,1,0:T(8,128)S(1)}, f32[1,128,256]{2,1,0:T(8,128)}, u32[]{:S(2)}) copy-start(f32[1,128,256]{2,1,0:T(8,128)} %dt_ref.1) | copy-start | bytes 393220
  72.3 25.5 %copy-start.1 = (f32[256]{0:T(256)S(1)}, f32[256]{0:T(256)}, u32[]{:S(2)}) copy-start(f32[256]{0:T(256)} %param.16) | copy-start | bytes 3076
  72.9 14.8 %collective-permute-start.12 = (s16[272,512]{1,0:T(8,128)(2,1)S(1)}, s16[272,512]{1,0:T(8,128)(2,1)S(1)}, u32[]{:S(2)}, u32[]{:S(2)}) collective-permute-start(s16[272,512]{1,0:T(8,128)(2,1)S(1)} %get-tuple-element.123), channel_id=1, source_target_pairs={{0,3},{1,0},{2,1},{3,2},{4,7},{5,4},{6,5},{7,6},{8,11},{9,8},{10,9... | collective-permute-start | bytes 835592 | tf_op jit(solution)/shard_map/ppermute | solution.py:450
  76.6 21.2 %collective-permute-start.15 = (f32[128,640]{1,0:T(8,128)S(1)}, f32[128,640]{1,0:T(8,128)S(1)}, u32[]{:S(2)}, u32[]{:S(2)}) collective-permute-start(f32[128,640]{1,0:T(8,128)S(1)} %get-tuple-element.131), channel_id=1, source_target_pairs={{0,12},{4,0},{8,4},{12,8},{1,13},{5,1},{9,5},{13,9},{2,14},{6,2},{... | collective-permute-start | bytes 983048 | tf_op jit(solution)/shard_map/ppermute | solution.py:449
  76.6 21.2 %collective-permute-start.16 = (f32[128,640]{1,0:T(8,128)S(1)}, f32[128,640]{1,0:T(8,128)S(1)}, u32[]{:S(2)}, u32[]{:S(2)}) collective-permute-start(f32[128,640]{1,0:T(8,128)S(1)} %get-tuple-element.132), channel_id=1, source_target_pairs={{0,8},{4,12},{8,0},{12,4},{1,9},{5,13},{9,1},{13,5},{2,10},{6,14},... | collective-permute-start | bytes 983048 | tf_op jit(solution)/shard_map/ppermute | solution.py:449
  77.8 20.0 %collective-permute-start.17 = (f32[128,640]{1,0:T(8,128)S(1)}, f32[128,640]{1,0:T(8,128)S(1)}, u32[]{:S(2)}, u32[]{:S(2)}) collective-permute-start(f32[128,640]{1,0:T(8,128)S(1)} %get-tuple-element.133), channel_id=1, source_target_pairs={{0,4},{4,8},{8,12},{12,0},{1,5},{5,9},{9,13},{13,1},{2,6},{6,10},{... | collective-permute-start | bytes 983048 | tf_op jit(solution)/shard_map/ppermute | solution.py:449
  80.5 8.1 %collective-permute-start.13 = (s16[272,512]{1,0:T(8,128)(2,1)S(1)}, s16[272,512]{1,0:T(8,128)(2,1)S(1)}, u32[]{:S(2)}, u32[]{:S(2)}) collective-permute-start(s16[272,512]{1,0:T(8,128)(2,1)S(1)} %get-tuple-element.124), channel_id=1, source_target_pairs={{0,2},{1,3},{2,0},{3,1},{4,6},{5,7},{6,4},{7,5},{8,10},{9,11},{10,... | collective-permute-start | bytes 835592 | tf_op jit(solution)/shard_map/ppermute | solution.py:450
  87.7 8.6 %collective-permute-start.14 = (s16[272,512]{1,0:T(8,128)(2,1)S(1)}, s16[272,512]{1,0:T(8,128)(2,1)S(1)}, u32[]{:S(2)}, u32[]{:S(2)}) collective-permute-start(s16[272,512]{1,0:T(8,128)(2,1)S(1)} %get-tuple-element.125), channel_id=1, source_target_pairs={{0,1},{1,2},{2,3},{3,0},{4,5},{5,6},{6,7},{7,4},{8,9},{9,10},{10,1... | collective-permute-start | bytes 835592 | tf_op jit(solution)/shard_map/ppermute | solution.py:450

commit v3 on v2

--- a/solution.py
+++ b/solution.py
@@ -80,7 +80,7 @@
     x_idx, y_idx, sign, adv, length, dt_hbm, rate_hbm, scale_hbm, cot_hbm, c_hbm, codes_hbm, *rest
 ):
     packs0, packs1 = rest[0:4], rest[4:8]
-    stp, ep_ref, fp_ref, dt_ref, rate_ref, scale_ref, cot_v, c_v, codes_v, sc_ref, sems = rest[8:19]
+    stp, ep_ref, fp_ref, dt_ref, rate_ref, scale_ref, sc_ref, sems = rest[8:16]
     me = x_idx[0]
     order = (2, 1, 3, 0)
     owners = [lax.rem(y_idx[0] + ROW - j, ROW) for j in range(ROW)]
@@ -95,14 +95,22 @@
     load_dt = start(dt_hbm, dt_ref)
     load_rate = start(rate_hbm, rate_ref)
     load_scale = start(scale_hbm, scale_ref)
-    loads = {}
+    stores = []
     for k in order:
         there = lax.rem(me + k, ROW)
-        at = pl.multiple_of(there * RW, RW)
-        loads[k] = start(cot_hbm.at[0, :, pl.ds(at, RW)], cot_v.at[k])
-    load_c = start(c_hbm.at[0], c_v)
-    load_codes = start(codes_hbm, codes_v)
-
+        for chunk, packs in enumerate((packs0, packs1)):
+            width = CWS[chunk]
+            for j in range(ROW):
+                at = pl.multiple_of(there * RW + owners[j] * OW + ATS[chunk], N)
+                stores.append(
+                    start(
+                        cot_hbm.at[0, :, pl.ds(at, width)],
+                        packs[k].at[:, pl.ds(j * width, width)],
+                    )
+                )
+        at = pl.multiple_of(there * 2 * N, 2 * N)
+        stores.append(start(c_hbm.at[0, :, pl.ds(at, 2 * N)], packs0[k].at[:, pl.ds(PWS[0], 2 * N)]))
+    stores.append(start(codes_hbm, stp.at[pl.ds(0, OW)]))
     load_dt.wait()
     load_rate.wait()
     step = softplus(dt_ref[0])
@@ -119,27 +127,9 @@
         ep_ref[q] = jnp.concatenate([e_hi[:, cols], e_lo[:, cols]], axis=1)
         fp_ref[q] = jnp.concatenate([f_hi[:, cols], f_lo[:, cols]], axis=1)
 
-    stores = []
-    load_c.wait()
     for k in order:
         there = lax.rem(me + k, ROW)
-        at = pl.multiple_of(there * 2 * N, 2 * N)
-        stores.append(start(c_v.at[:, pl.ds(at, 2 * N)], packs0[k].at[:, pl.ds(PWS[0], 2 * N)]))
         stores.append(start(ep_ref.at[there], packs0[k].at[:, pl.ds(PWS[0] + 2 * N, 2 * RH)]))
-    for k in order:
-        loads[k].wait()
-        for chunk, packs in enumerate((packs0, packs1)):
-            width = CWS[chunk]
-            for j in range(ROW):
-                at = pl.multiple_of(owners[j] * OW + ATS[chunk], N)
-                stores.append(
-                    start(
-                        cot_v.at[k, :, pl.ds(at, width)],
-                        packs[k].at[:, pl.ds(j * width, width)],
-                    )
-                )
-    load_codes.wait()
-    stores.append(start(codes_v, stp.at[pl.ds(0, OW)]))
 
     load_scale.wait()
     scale = scale_ref[...].astype(F32)
@@ -173,9 +163,6 @@
             pltpu.VMEM((1, TOK, H), F32),
             pltpu.VMEM((1, H), F32),
             pltpu.VMEM((OH, PS), BF16),
-            pltpu.VMEM((ROW, TOK, RW), BF16),
-            pltpu.VMEM((TOK, G * N), BF16),
-            pltpu.VMEM((OW, N), BF16),
             pltpu.VMEM((OH, N), BF16),
             pltpu.SemaphoreType.DMA((64,)),
         ],
@@ -341,7 +328,7 @@
     me = x_idx[0]
     lane = iota((TOK, H), 1) // RH
     q = jnp.zeros((TOK, H), F32)
-    for k, ret in enumerate((r0, r1, r2, r3)):
+    for k, ret in ((0, r0), (2, r1), (1, r2), (3, r3)):
         there = lax.rem(me + k, ROW)
         cols = pl.ds(pl.multiple_of(there * 2 * N, 2 * N), 2 * N)
         out_gc[0, :, cols] = (gc_ref[:, cols] + ret[:, : 2 * N]).astype(BF16)
@@ -444,11 +431,11 @@
     red0[0] = lax.ppermute(last, "ry", shift(-1))
     red0[1], red0[2], got1[0] = barrier((red0[1], red0[2], got1[0]))
     own1, send1, rets1 = owner(1, y_idx, got1, got0, states, rets0)
-    red0[0], a = barrier((red0[0], send1[0]))
-    b, c = send1[1:]
-    back = [rets1[0]] + [lax.ppermute(rets1[k], "rx", shift(-k)) for k in (1, 2, 3)]
-    red1 = [lax.ppermute(send, "ry", shift(-k)) for k, send in ((1, a), (2, b), (3, c))]
+    red0[0], *moved = barrier((red0[0], *rets1[1:], *send1))
+    back = [rets1[0]] + [lax.ppermute(moved[k - 1], "rx", shift(-k)) for k in (2, 1, 3)]
+    red1 = [lax.ppermute(moved[k + 2], "ry", shift(-k)) for k in (2, 1, 3)]
     grad_c, grad_dt = tokens(x_idx, dt_raw, rate, gc_part, q, sr, back)
+    grad_dt, own1 = barrier((grad_dt, own1))
     grad_state = state_out(own0, red0, own1, red1, stp)
     return grad_state.reshape(OH, PS, N), grad_b, grad_c, grad_dt
 

time: 99.2 us -> 94.1 us (0.949)
  waiting for transfers between devices: 19.6 us -> 14.1 us
  starting transfers between devices: 30.3 us -> 31.4 us
    ppermute x6, waiting for transfers between devices: 15.2 us -> 9.75 us  [the longest x3 7.97 us: per_device(): lax.ppermute(moved[k - 1], 'rx', shift(-k))]
    ppermute x6, starting transfers between devices: 8.23 us -> 9.37 us  [the longest x3 5.56 us: per_device(): red1 = [lax.ppermute(moved[k + 2], 'ry', shift(-k)) for k in (2, 1, 3)]]
  transfers between devices with their start and end apart: 18 -> 18, of which waited for: 5 -> 6; matrix products, arithmetic and copies ran while one was open for 0% -> 0% of each run, Pallas kernels for 42% -> 44%
where the time goes in v3:
time: 94.1 us; the launch traced here: 93.9 us
  Pallas kernels  45.8 us (49%)
  starting transfers between devices  31.4 us (33%)
  waiting for transfers between devices  14.1 us (15%)
  between operations  2.64 us (3%)
    pallas_call x3, Pallas kernels, within(): pl.pallas_call(functools.partial(within_kernel, first), grid=(last - firs...  28.9 us
    pallas_call x2, Pallas kernels, owner(): pl.pallas_call(functools.partial(owner_kernel, chunk), grid=(1,), out_sha...  10.8 us
    ppermute x3, waiting for transfers between devices, per_device(): lax.ppermute(moved[k - 1], 'rx', shift(-k))  7.97 us
    ppermute x3, starting transfers between devices, per_device(): red1 = [lax.ppermute(moved[k + 2], 'ry', shift(-k)) for k in (2, 1, 3)]  5.56 us
    ppermute x3, starting transfers between devices, per_device(): got0 = {k: lax.ppermute(packs0[k], 'rx', shift(k)) for k in (2, 1, 3)}  4.83 us
    ppermute x3, starting transfers between devices, per_device(): lax.ppermute(send1[k - 1], 'rx', shift(k))  4.51 us
    ppermute x3, waiting for transfers between devices, per_device(): lax.ppermute(send1[k - 1], 'rx', shift(k))  3.81 us
    ppermute x3, starting transfers between devices, per_device(): lax.ppermute(moved[k - 1], 'rx', shift(-k))  3.81 us
  transfers between devices with their start and end apart: 18, of which 6 were waited for; matrix products, arithmetic and copies ran while one was open for 0% of the time, Pallas kernels for 44%

profile of v3, /device:TPU:130, one launch (start us, length us, event | category | flops | bytes accessed | tf_op | source)
XLA Modules:
  0.0 93.9 jit_solution(7719450742067718059)
XLA Ops:
  2.6 3.3 %prep.1 = (bf16[128,2688]{1,0:T(8,128)(2,1)S(1)}, bf16[128,2688]{1,0:T(8,128)(2,1)S(1)}, bf16[128,2688]{1,0:T(8,128)(2,1)S(1)}, bf16[128,2688]{1,0:T(8,128)(2,1)...) custom-call(s32[1]{0:T(128)} %bitcast.1.x_idx, ...), custom_call_target="tpu_custom_call" | custom-call | flops 1000 | bytes 1000 | tf_op jit(solution)/shard_map/prep/pallas_call | solution.py:154
  5.8 1.6 %collective-permute-start.2 = (bf16[128,2688]{1,0:T(8,128)(2,1)S(1)}, bf16[128,2688]{1,0:T(8,128)(2,1)S(1)}, u32[]{:S(2)}, u32[]{:S(2)}) collective-permute-start(bf16[128,2688]{1,0:T(8,128)(2,1)S(1)} %get-tuple-element.92), channel_id=1, source_target_pairs={{0,4},{4,8},{8,12},{12,0},{1,5},{5,9},{9,13},{13,1},{2,6},{6,10},{... | collective-permute-start | bytes 2064392 | tf_op jit(solution)/shard_map/ppermute | solution.py:414
  7.4 1.1 %collective-permute-start.3 = (bf16[128,2688]{1,0:T(8,128)(2,1)S(1)}, bf16[128,2688]{1,0:T(8,128)(2,1)S(1)}, u32[]{:S(2)}, u32[]{:S(2)}) collective-permute-start(bf16[128,2688]{1,0:T(8,128)(2,1)S(1)} %get-tuple-element.93), channel_id=1, source_target_pairs={{0,8},{4,12},{8,0},{12,4},{1,9},{5,13},{9,1},{13,5},{2,10},{6,14},... | collective-permute-start | bytes 2064392 | tf_op jit(solution)/shard_map/ppermute | solution.py:414
  8.5 3.0 %collective-permute-start.1 = (bf16[1040,256]{1,0:T(8,128)(2,1)S(1)}, bf16[1040,256]{1,0:T(8,128)(2,1)S(1)}, u32[]{:S(2)}, u32[]{:S(2)}) collective-permute-start(bf16[1040,256]{1,0:T(8,128)(2,1)S(1)} %get-tuple-element.96.refs_12_.refs_16_.refs_8_), channel_id=1, source_target_pairs={{0,3},{1,0},{2,1},{3,2},{4,7},{5,4},{6,5},{7,6},{8,11},{9,8},{10,9... | collective-permute-start | bytes 1597448 | tf_op jit(solution)/shard_map/ppermute | solution.py:417
  11.5 0.0 collective-permute-start
  11.5 2.2 %collective-permute-start.4 = (bf16[128,2688]{1,0:T(8,128)(2,1)S(1)}, bf16[128,2688]{1,0:T(8,128)(2,1)S(1)}, u32[]{:S(2)}, u32[]{:S(2)}) collective-permute-start(bf16[128,2688]{1,0:T(8,128)(2,1)S(1)} %get-tuple-element.94), channel_id=1, source_target_pairs={{0,12},{4,0},{8,4},{12,8},{1,13},{5,1},{9,5},{13,9},{2,14},{6,2},{... | collective-permute-start | bytes 2064392 | tf_op jit(solution)/shard_map/ppermute | solution.py:414
  13.7 13.5 %within0.1 = (bf16[1,128,2048]{2,1,0:T(8,128)(2,1)}, f32[128,2048]{1,0:T(8,128)S(1)}, f32[4,128,128]{2,1,0:T(8,128)S(1)}, f32[4,128,128]{2,1,0:T(8,128)S(1)}) custom-call(bf16[1,128,16384]{2,1,0:T(8,128)(2,1)} %x_ref.5, bf16[1,128,16384]{2,1,0:T(8,128)(2,1)} %cot_ref.5, bf16[1,128,2048]{2,1,0:T(8,128)(2,1)} %b_ref.5, bf16[1,128,2048]{2,1,0:T(8,128)(2,1)} %c_ref.5, ...), custom_call_target="tpu_custom_call" | custom-call | flops 1000 | bytes 1000 | tf_op jit(solution)/shard_map/within0/pallas_call | solution.py:233
  27.2 0.0 collective-permute-done.1.refs_15_.refs_19_
  27.2 0.0 collective-permute-done.refs_13_.refs_17_
  27.2 2.3 %collective-permute-start.5 = (bf16[1040,256]{1,0:T(8,128)(2,1)S(1)}, bf16[1040,256]{1,0:T(8,128)(2,1)S(1)}, u32[]{:S(2)}, u32[]{:S(2)}) collective-permute-start(bf16[1040,256]{1,0:T(8,128)(2,1)S(1)} %get-tuple-element.96.refs_12_.refs_16_.refs_8_), channel_id=1, source_target_pairs={{0,2},{1,3},{2,0},{3,1},{4,6},{5,7},{6,4},{7,5},{8,10},{9,11},{10,... | collective-permute-start | bytes 1597448 | tf_op jit(solution)/shard_map/ppermute | solution.py:420
  29.5 7.7 %within4.1 = (bf16[1,128,2048]{2,1,0:T(8,128)(2,1)}, f32[128,2048]{1,0:T(8,128)S(1)}, f32[4,128,128]{2,1,0:T(8,128)S(1)}, f32[4,128,128]{2,1,0:T(8,128)S(1)}) custom-call(bf16[1,128,16384]{2,1,0:T(8,128)(2,1)} %x_ref.5, bf16[1,128,16384]{2,1,0:T(8,128)(2,1)} %cot_ref.5, ...), custom_call_target="tpu_custom_call", output_to_operand_aliasing={{0}: (6, {}), {1}: (7, {}), {2}: (8, {}), {3}: (9, {})} | custom-call | flops 1000 | bytes 1000 | tf_op jit(solution)/shard_map/within4/pallas_call | solution.py:233
  37.2 0.0 collective-permute-start.6
  37.2 0.0 collective-permute-done.2.refs_1_.refs_5_.refs_9_
  37.2 3.5 %collective-permute-start.7 = (bf16[128,2048]{1,0:T(8,128)(2,1)S(1)}, bf16[128,2048]{1,0:T(8,128)(2,1)S(1)}, u32[]{:S(2)}, u32[]{:S(2)}) collective-permute-start(bf16[128,2048]{1,0:T(8,128)(2,1)S(1)} %get-tuple-element.111), channel_id=1, source_target_pairs={{0,8},{4,12},{8,0},{12,4},{1,9},{5,13},{9,1},{13,5},{2,10},{6,14},... | collective-permute-start | bytes 1572872 | tf_op jit(solution)/shard_map/ppermute | solution.py:423
  40.7 0.0 collective-permute-done.3.refs_2_.refs_6_.refs_10_
  40.7 1.0 %collective-permute-start.8 = (bf16[128,2048]{1,0:T(8,128)(2,1)S(1)}, bf16[128,2048]{1,0:T(8,128)(2,1)S(1)}, u32[]{:S(2)}, u32[]{:S(2)}) collective-permute-start(bf16[128,2048]{1,0:T(8,128)(2,1)S(1)} %get-tuple-element.112), channel_id=1, source_target_pairs={{0,12},{4,0},{8,4},{12,8},{1,13},{5,1},{9,5},{13,9},{2,14},{6,2},{... | collective-permute-start | bytes 1572872 | tf_op jit(solution)/shard_map/ppermute | solution.py:423
  41.7 0.0 collective-permute-done.4.refs_3_.refs_7_.refs_11_
  41.7 0.0 collective-permute-done.5.refs_14_.refs_18_
  41.7 5.4 %owner0.1 = (f32[256,512]{1,0:T(8,128)S(1)}, s16[272,512]{1,0:T(8,128)(2,1)S(1)}, s16[272,512]{1,0:T(8,128)(2,1)S(1)}, s16[272,512]{1,0:T(8,128)(2,1)S(1)}, f32[...) custom-call(s32[1]{0:T(128)} %bitcast.y_idx, ...), custom_call_target="tpu_custom_call" | custom-call | flops 1000 | bytes 1000 | tf_op jit(solution)/shard_map/owner0/pallas_call | solution.py:306
  47.1 3.7 %collective-permute-start.10 = (s16[272,512]{1,0:T(8,128)(2,1)S(1)}, s16[272,512]{1,0:T(8,128)(2,1)S(1)}, u32[]{:S(2)}, u32[]{:S(2)}) collective-permute-start(s16[272,512]{1,0:T(8,128)(2,1)S(1)} %get-tuple-element.114), channel_id=1, source_target_pairs={{0,2},{1,3},{2,0},{3,1},{4,6},{5,7},{6,4},{7,5},{8,10},{9,11},{10,... | collective-permute-start | bytes 835592 | tf_op jit(solution)/shard_map/ppermute | solution.py:426
  50.8 0.7 collective-permute-start.11
  51.5 7.7 %within6.1 = (bf16[1,128,2048]{2,1,0:T(8,128)(2,1)}, f32[128,2048]{1,0:T(8,128)S(1)}, f32[4,128,128]{2,1,0:T(8,128)S(1)}, f32[4,128,128]{2,1,0:T(8,128)S(1)}) custom-call(bf16[1,128,16384]{2,1,0:T(8,128)(2,1)} %x_ref.5, bf16[1,128,16384]{2,1,0:T(8,128)(2,1)} %cot_ref.5, ...), custom_call_target="tpu_custom_call", output_to_operand_aliasing={{0}: (6, {}), {1}: (7, {}), {2}: (8, {}), {3}: (9, {})} | custom-call | flops 1000 | bytes 1000 | tf_op jit(solution)/shard_map/within6/pallas_call | solution.py:233
  59.2 0.0 collective-permute-done.6.refs_1_
  59.2 0.0 collective-permute-done.7.refs_2_
  59.2 3.8 %collective-permute-done.8.refs_3_ = bf16[128,2048]{1,0:T(8,128)(2,1)S(1)} collective-permute-done((bf16[128,2048]{1,0:T(8,128)(2,1)S(1)}, bf16[128,2048]{1,0:T(8,128)(2,1)S(1)}, u32[]{:S(2)}, u32[]{:S(2)}) %collective-permute-start.8) | collective-permute-done | bytes 524320 | tf_op jit(solution)/shard_map/ppermute | solution.py:423
  63.0 3.0 %collective-permute-start.9 = (s16[272,512]{1,0:T(8,128)(2,1)S(1)}, s16[272,512]{1,0:T(8,128)(2,1)S(1)}, u32[]{:S(2)}, u32[]{:S(2)}) collective-permute-start(s16[272,512]{1,0:T(8,128)(2,1)S(1)} %get-tuple-element.113), channel_id=1, source_target_pairs={{0,3},{1,0},{2,1},{3,2},{4,7},{5,4},{6,5},{7,6},{8,11},{9,8},{10,9... | collective-permute-start | bytes 835592 | tf_op jit(solution)/shard_map/ppermute | solution.py:431
  66.0 0.0 collective-permute-done.10.refs_2_
  66.1 0.0 collective-permute-done.11.refs_3_
  66.1 0.0 copy-start
  66.1 0.0 copy-start.1
  66.1 5.4 %owner1.1 = (f32[256,512]{1,0:T(8,128)S(1)}, s16[272,512]{1,0:T(8,128)(2,1)S(1)}, s16[272,512]{1,0:T(8,128)(2,1)S(1)}, s16[272,512]{1,0:T(8,128)(2,1)S(1)}, f32[...) custom-call(s32[1]{0:T(128)} %bitcast.y_idx, ...), custom_call_target="tpu_custom_call" | custom-call | flops 1000 | bytes 1000 | tf_op jit(solution)/shard_map/owner1/pallas_call | solution.py:306
  71.5 0.5 collective-permute-done.9.refs_1_
  72.0 1.8 %collective-permute-start.12 = (f32[128,640]{1,0:T(8,128)S(1)}, f32[128,640]{1,0:T(8,128)S(1)}, u32[]{:S(2)}, u32[]{:S(2)}) collective-permute-start(f32[128,640]{1,0:T(8,128)S(1)} %get-tuple-element.138), channel_id=1, source_target_pairs={{0,8},{4,12},{8,0},{12,4},{1,9},{5,13},{9,1},{13,5},{2,10},{6,14},... | collective-permute-start | bytes 983048 | tf_op jit(solution)/shard_map/ppermute | solution.py:435
  73.8 0.5 collective-permute-start.13
  74.3 1.5 %collective-permute-start.14 = (f32[128,640]{1,0:T(8,128)S(1)}, f32[128,640]{1,0:T(8,128)S(1)}, u32[]{:S(2)}, u32[]{:S(2)}) collective-permute-start(f32[128,640]{1,0:T(8,128)S(1)} %get-tuple-element.140), channel_id=1, source_target_pairs={{0,4},{4,8},{8,12},{12,0},{1,5},{5,9},{9,13},{13,1},{2,6},{6,10},{... | collective-permute-start | bytes 983048 | tf_op jit(solution)/shard_map/ppermute | solution.py:435
  75.8 2.1 %collective-permute-start.15 = (s16[272,512]{1,0:T(8,128)(2,1)S(1)}, s16[272,512]{1,0:T(8,128)(2,1)S(1)}, u32[]{:S(2)}, u32[]{:S(2)}) collective-permute-start(s16[272,512]{1,0:T(8,128)(2,1)S(1)} %get-tuple-element.144), channel_id=1, source_target_pairs={{0,2},{1,3},{2,0},{3,1},{4,6},{5,7},{6,4},{7,5},{8,10},{9,11},{10,... | collective-permute-start | bytes 835592 | tf_op jit(solution)/shard_map/ppermute | solution.py:436
  78.0 2.3 %collective-permute-start.16 = (s16[272,512]{1,0:T(8,128)(2,1)S(1)}, s16[272,512]{1,0:T(8,128)(2,1)S(1)}, u32[]{:S(2)}, u32[]{:S(2)}) collective-permute-start(s16[272,512]{1,0:T(8,128)(2,1)S(1)} %get-tuple-element.145), channel_id=1, source_target_pairs={{0,3},{1,0},{2,1},{3,2},{4,7},{5,4},{6,5},{7,6},{8,11},{9,8},{10,9... | collective-permute-start | bytes 835592 | tf_op jit(solution)/shard_map/ppermute | solution.py:436
  80.3 3.9 %collective-permute-done.12.r1 = f32[128,640]{1,0:T(8,128)S(1)} collective-permute-done((f32[128,640]{1,0:T(8,128)S(1)}, f32[128,640]{1,0:T(8,128)S(1)}, u32[]{:S(2)}, u32[]{:S(2)}) %collective-permute-start.12) | collective-permute-done | bytes 327712 | tf_op jit(solution)/shard_map/ppermute | solution.py:435
  84.2 1.1 %collective-permute-start.17 = (s16[272,512]{1,0:T(8,128)(2,1)S(1)}, s16[272,512]{1,0:T(8,128)(2,1)S(1)}, u32[]{:S(2)}, u32[]{:S(2)}) collective-permute-start(s16[272,512]{1,0:T(8,128)(2,1)S(1)} %get-tuple-element.146), channel_id=1, source_target_pairs={{0,1},{1,2},{2,3},{3,0},{4,5},{5,6},{6,7},{7,4},{8,9},{9,10},{10,1... | collective-permute-start | bytes 835592 | tf_op jit(solution)/shard_map/ppermute | solution.py:436
  85.4 4.0 %collective-permute-done.13.r2 = f32[128,640]{1,0:T(8,128)S(1)} collective-permute-done((f32[128,640]{1,0:T(8,128)S(1)}, f32[128,640]{1,0:T(8,128)S(1)}, u32[]{:S(2)}, u32[]{:S(2)}) %collective-permute-start.13) | collective-permute-done | bytes 327712 | tf_op jit(solution)/shard_map/ppermute | solution.py:435
  89.4 0.0 collective-permute-done.14.r3
  89.4 0.0 copy-done
  89.4 0.0 copy-done.1
  89.4 1.2 %tokens.1 = (bf16[1,128,2048]{2,1,0:T(8,128)(2,1)}, f32[1,128,256]{2,1,0:T(8,128)}) custom-call(s32[1]{0:T(128)} %bitcast.1.x_idx, f32[1,128,256]{2,1,0:T(8,128)S(1)} %copy-done, f32[1,256]{1,0:T(1,128)S(1)} %bitcast.6, f32[128,2048]{1,0:T(8,128)S(1)} %get-tuple-element.134.gc_ref, f32[4,128,128]{2,1,0:T(8,128)S(1)} %get-tuple-element.135.q_ref, ...), custom_call_target="tpu_custom_call" | custom-call | flops 1000 | bytes 1000 | tf_op jit(solution)/shard_map/tokens/pallas_call | solution.py:353
  90.6 0.0 collective-permute-done.15.refs_5_
  90.6 0.1 collective-permute-done.16.refs_6_
  90.8 1.6 %collective-permute-done.17.refs_7_ = s16[272,512]{1,0:T(8,128)(2,1)S(1)} collective-permute-done((s16[272,512]{1,0:T(8,128)(2,1)S(1)}, s16[272,512]{1,0:T(8,128)(2,1)S(1)}, u32[]{:S(2)}, u32[]{:S(2)}) %collective-permute-start.17) | collective-permute-done | bytes 278560 | tf_op jit(solution)/shard_map/ppermute | solution.py:436
  92.4 1.5 %state_out.1 = f32[1024,256]{1,0:T(8,128)} custom-call(f32[256,512]{1,0:T(8,128)S(1)} %get-tuple-element.98.refs_0_, s16[272,512]{1,0:T(8,128)(2,1)S(1)} %collective-permute-done.9.refs_1_, s16[272,512]{1,0:T(8,128)(2,1)S(1)} %collective-permute-done.10.refs_2_, s16[272,512]{1,0:T(8,128)(2,1)S(1)} %collective-permute-done.11.refs_3_, ...), custom_call_target="tpu_custom_call" | custom-call | flops 1000 | bytes 1000 | tf_op jit(solution)/shard_map/state_out/pallas_call | solution.py:385
Async XLA Ops:
  5.8 31.4 %collective-permute-start.2 = (bf16[128,2688]{1,0:T(8,128)(2,1)S(1)}, bf16[128,2688]{1,0:T(8,128)(2,1)S(1)}, u32[]{:S(2)}, u32[]{:S(2)}) collective-permute-start(bf16[128,2688]{1,0:T(8,128)(2,1)S(1)} %get-tuple-element.92), channel_id=1, source_target_pairs={{0,4},{4,8},{8,12},{12,0},{1,5},{5,9},{9,13},{13,1},{2,6},{6,10},{... | collective-permute-start | bytes 2064392 | tf_op jit(solution)/shard_map/ppermute | solution.py:414
  7.4 33.3 %collective-permute-start.3 = (bf16[128,2688]{1,0:T(8,128)(2,1)S(1)}, bf16[128,2688]{1,0:T(8,128)(2,1)S(1)}, u32[]{:S(2)}, u32[]{:S(2)}) collective-permute-start(bf16[128,2688]{1,0:T(8,128)(2,1)S(1)} %get-tuple-element.93), channel_id=1, source_target_pairs={{0,8},{4,12},{8,0},{12,4},{1,9},{5,13},{9,1},{13,5},{2,10},{6,14},... | collective-permute-start | bytes 2064392 | tf_op jit(solution)/shard_map/ppermute | solution.py:414
  8.5 18.7 %collective-permute-start.1 = (bf16[1040,256]{1,0:T(8,128)(2,1)S(1)}, bf16[1040,256]{1,0:T(8,128)(2,1)S(1)}, u32[]{:S(2)}, u32[]{:S(2)}) collective-permute-start(bf16[1040,256]{1,0:T(8,128)(2,1)S(1)} %get-tuple-element.96.refs_12_.refs_16_.refs_8_), channel_id=1, source_target_pairs={{0,3},{1,0},{2,1},{3,2},{4,7},{5,4},{6,5},{7,6},{8,11},{9,8},{10,9... | collective-permute-start | bytes 1597448 | tf_op jit(solution)/shard_map/ppermute | solution.py:417
  11.5 15.6 %collective-permute-start = (bf16[1040,256]{1,0:T(8,128)(2,1)S(1)}, bf16[1040,256]{1,0:T(8,128)(2,1)S(1)}, u32[]{:S(2)}, u32[]{:S(2)}) collective-permute-start(bf16[1040,256]{1,0:T(8,128)(2,1)S(1)} %get-tuple-element.96.refs_12_.refs_16_.refs_8_), channel_id=1, source_target_pairs={{0,1},{1,2},{2,3},{3,0},{4,5},{5,6},{6,7},{7,4},{8,9},{9,10},{10,1... | collective-permute-start | bytes 1597448 | tf_op jit(solution)/shard_map/ppermute | solution.py:417
  11.5 30.2 %collective-permute-start.4 = (bf16[128,2688]{1,0:T(8,128)(2,1)S(1)}, bf16[128,2688]{1,0:T(8,128)(2,1)S(1)}, u32[]{:S(2)}, u32[]{:S(2)}) collective-permute-start(bf16[128,2688]{1,0:T(8,128)(2,1)S(1)} %get-tuple-element.94), channel_id=1, source_target_pairs={{0,12},{4,0},{8,4},{12,8},{1,13},{5,1},{9,5},{13,9},{2,14},{6,2},{... | collective-permute-start | bytes 2064392 | tf_op jit(solution)/shard_map/ppermute | solution.py:414
  27.2 14.5 %collective-permute-start.5 = (bf16[1040,256]{1,0:T(8,128)(2,1)S(1)}, bf16[1040,256]{1,0:T(8,128)(2,1)S(1)}, u32[]{:S(2)}, u32[]{:S(2)}) collective-permute-start(bf16[1040,256]{1,0:T(8,128)(2,1)S(1)} %get-tuple-element.96.refs_12_.refs_16_.refs_8_), channel_id=1, source_target_pairs={{0,2},{1,3},{2,0},{3,1},{4,6},{5,7},{6,4},{7,5},{8,10},{9,11},{10,... | collective-permute-start | bytes 1597448 | tf_op jit(solution)/shard_map/ppermute | solution.py:420
  37.2 22.0 %collective-permute-start.6 = (bf16[128,2048]{1,0:T(8,128)(2,1)S(1)}, bf16[128,2048]{1,0:T(8,128)(2,1)S(1)}, u32[]{:S(2)}, u32[]{:S(2)}) collective-permute-start(bf16[128,2048]{1,0:T(8,128)(2,1)S(1)} %get-tuple-element.110), channel_id=1, source_target_pairs={{0,4},{4,8},{8,12},{12,0},{1,5},{5,9},{9,13},{13,1},{2,6},{6,10},{... | collective-permute-start | bytes 1572872 | tf_op jit(solution)/shard_map/ppermute | solution.py:423
  37.2 22.0 %collective-permute-start.7 = (bf16[128,2048]{1,0:T(8,128)(2,1)S(1)}, bf16[128,2048]{1,0:T(8,128)(2,1)S(1)}, u32[]{:S(2)}, u32[]{:S(2)}) collective-permute-start(bf16[128,2048]{1,0:T(8,128)(2,1)S(1)} %get-tuple-element.111), channel_id=1, source_target_pairs={{0,8},{4,12},{8,0},{12,4},{1,9},{5,13},{9,1},{13,5},{2,10},{6,14},... | collective-permute-start | bytes 1572872 | tf_op jit(solution)/shard_map/ppermute | solution.py:423
  40.7 22.3 %collective-permute-start.8 = (bf16[128,2048]{1,0:T(8,128)(2,1)S(1)}, bf16[128,2048]{1,0:T(8,128)(2,1)S(1)}, u32[]{:S(2)}, u32[]{:S(2)}) collective-permute-start(bf16[128,2048]{1,0:T(8,128)(2,1)S(1)} %get-tuple-element.112), channel_id=1, source_target_pairs={{0,12},{4,0},{8,4},{12,8},{1,13},{5,1},{9,5},{13,9},{2,14},{6,2},{... | collective-permute-start | bytes 1572872 | tf_op jit(solution)/shard_map/ppermute | solution.py:423
  47.1 18.9 %collective-permute-start.10 = (s16[272,512]{1,0:T(8,128)(2,1)S(1)}, s16[272,512]{1,0:T(8,128)(2,1)S(1)}, u32[]{:S(2)}, u32[]{:S(2)}) collective-permute-start(s16[272,512]{1,0:T(8,128)(2,1)S(1)} %get-tuple-element.114), channel_id=1, source_target_pairs={{0,2},{1,3},{2,0},{3,1},{4,6},{5,7},{6,4},{7,5},{8,10},{9,11},{10,... | collective-permute-start | bytes 835592 | tf_op jit(solution)/shard_map/ppermute | solution.py:426
  50.8 15.2 %collective-permute-start.11 = (s16[272,512]{1,0:T(8,128)(2,1)S(1)}, s16[272,512]{1,0:T(8,128)(2,1)S(1)}, u32[]{:S(2)}, u32[]{:S(2)}) collective-permute-start(s16[272,512]{1,0:T(8,128)(2,1)S(1)} %get-tuple-element.115), channel_id=1, source_target_pairs={{0,1},{1,2},{2,3},{3,0},{4,5},{5,6},{6,7},{7,4},{8,9},{9,10},{10,1... | collective-permute-start | bytes 835592 | tf_op jit(solution)/shard_map/ppermute | solution.py:426
  63.0 9.0 %collective-permute-start.9 = (s16[272,512]{1,0:T(8,128)(2,1)S(1)}, s16[272,512]{1,0:T(8,128)(2,1)S(1)}, u32[]{:S(2)}, u32[]{:S(2)}) collective-permute-start(s16[272,512]{1,0:T(8,128)(2,1)S(1)} %get-tuple-element.113), channel_id=1, source_target_pairs={{0,3},{1,0},{2,1},{3,2},{4,7},{5,4},{6,5},{7,6},{8,11},{9,8},{10,9... | collective-permute-start | bytes 835592 | tf_op jit(solution)/shard_map/ppermute | solution.py:431
  66.1 23.3 %copy-start = (f32[1,128,256]{2,1,0:T(8,128)S(1)}, f32[1,128,256]{2,1,0:T(8,128)}, u32[]{:S(2)}) copy-start(f32[1,128,256]{2,1,0:T(8,128)} %dt_ref.1) | copy-start | bytes 393220
  66.1 23.3 %copy-start.1 = (f32[256]{0:T(256)S(1)}, f32[256]{0:T(256)}, u32[]{:S(2)}) copy-start(f32[256]{0:T(256)} %param.16) | copy-start | bytes 3076
  72.0 12.2 %collective-permute-start.12 = (f32[128,640]{1,0:T(8,128)S(1)}, f32[128,640]{1,0:T(8,128)S(1)}, u32[]{:S(2)}, u32[]{:S(2)}) collective-permute-start(f32[128,640]{1,0:T(8,128)S(1)} %get-tuple-element.138), channel_id=1, source_target_pairs={{0,8},{4,12},{8,0},{12,4},{1,9},{5,13},{9,1},{13,5},{2,10},{6,14},... | collective-permute-start | bytes 983048 | tf_op jit(solution)/shard_map/ppermute | solution.py:435
  73.8 15.6 %collective-permute-start.13 = (f32[128,640]{1,0:T(8,128)S(1)}, f32[128,640]{1,0:T(8,128)S(1)}, u32[]{:S(2)}, u32[]{:S(2)}) collective-permute-start(f32[128,640]{1,0:T(8,128)S(1)} %get-tuple-element.139), channel_id=1, source_target_pairs={{0,12},{4,0},{8,4},{12,8},{1,13},{5,1},{9,5},{13,9},{2,14},{6,2},{... | collective-permute-start | bytes 983048 | tf_op jit(solution)/shard_map/ppermute | solution.py:435
  74.3 15.1 %collective-permute-start.14 = (f32[128,640]{1,0:T(8,128)S(1)}, f32[128,640]{1,0:T(8,128)S(1)}, u32[]{:S(2)}, u32[]{:S(2)}) collective-permute-start(f32[128,640]{1,0:T(8,128)S(1)} %get-tuple-element.140), channel_id=1, source_target_pairs={{0,4},{4,8},{8,12},{12,0},{1,5},{5,9},{9,13},{13,1},{2,6},{6,10},{... | collective-permute-start | bytes 983048 | tf_op jit(solution)/shard_map/ppermute | solution.py:435
  75.8 14.8 %collective-permute-start.15 = (s16[272,512]{1,0:T(8,128)(2,1)S(1)}, s16[272,512]{1,0:T(8,128)(2,1)S(1)}, u32[]{:S(2)}, u32[]{:S(2)}) collective-permute-start(s16[272,512]{1,0:T(8,128)(2,1)S(1)} %get-tuple-element.144), channel_id=1, source_target_pairs={{0,2},{1,3},{2,0},{3,1},{4,6},{5,7},{6,4},{7,5},{8,10},{9,11},{10,... | collective-permute-start | bytes 835592 | tf_op jit(solution)/shard_map/ppermute | solution.py:436
  78.0 12.8 %collective-permute-start.16 = (s16[272,512]{1,0:T(8,128)(2,1)S(1)}, s16[272,512]{1,0:T(8,128)(2,1)S(1)}, u32[]{:S(2)}, u32[]{:S(2)}) collective-permute-start(s16[272,512]{1,0:T(8,128)(2,1)S(1)} %get-tuple-element.145), channel_id=1, source_target_pairs={{0,3},{1,0},{2,1},{3,2},{4,7},{5,4},{6,5},{7,6},{8,11},{9,8},{10,9... | collective-permute-start | bytes 835592 | tf_op jit(solution)/shard_map/ppermute | solution.py:436
  84.2 8.2 %collective-permute-start.17 = (s16[272,512]{1,0:T(8,128)(2,1)S(1)}, s16[272,512]{1,0:T(8,128)(2,1)S(1)}, u32[]{:S(2)}, u32[]{:S(2)}) collective-permute-start(s16[272,512]{1,0:T(8,128)(2,1)S(1)} %get-tuple-element.146), channel_id=1, source_target_pairs={{0,1},{1,2},{2,3},{3,0},{4,5},{5,6},{6,7},{7,4},{8,9},{9,10},{10,1... | collective-permute-start | bytes 835592 | tf_op jit(solution)/shard_map/ppermute | solution.py:436

commit v4 on v3

--- a/solution.py
+++ b/solution.py
@@ -288,11 +288,12 @@
             sends[k - 1][N:] = jnp.broadcast_to(level.astype(jnp.int32), (PAD, width)).astype(jnp.int16)
         gc = dot(d_hi, codes) + dot(d_lo, codes)
         p_hi, p_lo = split2(dy * dot_nt(c, codes))
-        q = dot_nt(p_hi, sel) + dot_nt(p_lo, sel)
+        q = dot_nt(sel, p_hi) + dot_nt(sel, p_lo)
         for r in range(ROW):
             rows = slice(r * TOK, (r + 1) * TOK)
-            rets[r][:, half] += gc[rows]
-            rets[r][:, 2 * N :] += q[rows]
+            rets[r][:TOK, half] += gc[rows]
+            for b in range(ROW):
+                rets[r][TOK:, b * TOK : (b + 1) * TOK] += q[b * OH : (b + 1) * OH, rows]
 
 
 def owner(chunk, y_idx, cots, packs0, states, olds):
@@ -300,8 +301,8 @@
     cot_spec = pl.BlockSpec((TOK, PWS[chunk]), lambda i: (0, 0))
     c_spec = pl.BlockSpec((TOK, 2 * N), lambda i: (0, PWS[0] // (2 * N)))
     e_spec = pl.BlockSpec((TOK, 2 * RH), lambda i: (0, (PWS[0] + 2 * N) // (2 * RH)))
-    ret_spec = pl.BlockSpec((TOK, 2 * N + 2 * RH), lambda i: (0, 0))
-    ret_shape = jax.ShapeDtypeStruct((TOK, 2 * N + 2 * RH), F32)
+    ret_spec = pl.BlockSpec((TOK + OH, 2 * N), lambda i: (0, 0))
+    ret_shape = jax.ShapeDtypeStruct((TOK + OH, 2 * N), F32)
     send_spec = pl.BlockSpec((N + PAD, width), lambda i: (0, 0))
     outs = pl.pallas_call(
         functools.partial(owner_kernel, chunk),
@@ -331,8 +332,9 @@
     for k, ret in ((0, r0), (2, r1), (1, r2), (3, r3)):
         there = lax.rem(me + k, ROW)
         cols = pl.ds(pl.multiple_of(there * 2 * N, 2 * N), 2 * N)
-        out_gc[0, :, cols] = (gc_ref[:, cols] + ret[:, : 2 * N]).astype(BF16)
-        held = ret[:, 2 * N :]
+        out_gc[0, :, cols] = (gc_ref[:, cols] + ret[:TOK]).astype(BF16)
+        rows = [ret[TOK:, b * TOK : (b + 1) * TOK] for b in range(ROW)]
+        held = jnp.concatenate(rows + rows, axis=0).T
         q = jnp.where(lane == there, jnp.concatenate([held, held], axis=1), q)
     sr = jnp.zeros((TOK, H), F32)
     for b in range(ROW):
@@ -414,10 +416,10 @@
     got0 = {k: lax.ppermute(packs0[k], "rx", shift(k)) for k in (2, 1, 3)}
     got0[0] = packs0[0]
     got0 = [got0[k] for k in range(ROW)]
-    states = [stp, lax.ppermute(stp, "ry", shift(1)), None, lax.ppermute(stp, "ry", shift(3))]
+    far = lax.ppermute(stp, "ry", shift(2))
     first = within(0, 4, *args, ())
-    gc_part, state, states[1], states[3] = barrier((first[1], stp, states[1], states[3]))
-    states[2] = lax.ppermute(state, "ry", shift(2))
+    gc_part, state, far = barrier((first[1], stp, far))
+    states = [stp, lax.ppermute(state, "ry", shift(1)), far, lax.ppermute(state, "ry", shift(3))]
     second = within(4, 6, *args, (first[0], gc_part, *first[2:]))
     gc_part, *send1 = barrier((second[1], *packs1[1:]))
     got1 = [packs1[0]] + [lax.ppermute(send1[k - 1], "rx", shift(k)) for k in (1, 2, 3)]

time: 94.1 us -> 93.5 us (level)
  starting transfers between devices: 31.4 us -> 29.8 us
    ppermute x3, starting transfers between devices: 5.56 us -> 4.51 us  [per_device(): red1 = [lax.ppermute(moved[k + 2], 'ry', shift(-k)) for k in (2, 1, 3)]]
  transfers between devices with their start and end apart: 18 -> 18, of which waited for: 6 -> 7; matrix products, arithmetic and copies ran while one was open for 0% -> 0% of each run, Pallas kernels for 44% -> 44%
where the time goes in v4:
time: 93.5 us; the launch traced here: 93.1 us
  Pallas kernels  45.6 us (49%)
  starting transfers between devices  29.8 us (32%)
  waiting for transfers between devices  15 us (16%)
  between operations  2.65 us (3%)
    pallas_call x3, Pallas kernels, within(): pl.pallas_call(functools.partial(within_kernel, first), grid=(last - firs...  28.9 us
    pallas_call x2, Pallas kernels, owner(): pl.pallas_call(functools.partial(owner_kernel, chunk), grid=(1,), out_sha...  10.6 us
    ppermute x3, waiting for transfers between devices, per_device(): lax.ppermute(moved[k - 1], 'rx', shift(-k))  7.56 us
    ppermute x3, starting transfers between devices, per_device(): got0 = {k: lax.ppermute(packs0[k], 'rx', shift(k)) for k in (2, 1, 3)}  4.83 us
    ppermute x3, starting transfers between devices, per_device(): lax.ppermute(send1[k - 1], 'rx', shift(k))  4.6 us
    ppermute x3, starting transfers between devices, per_device(): red1 = [lax.ppermute(moved[k + 2], 'ry', shift(-k)) for k in (2, 1, 3)]  4.51 us
    ppermute x3, waiting for transfers between devices, per_device(): lax.ppermute(send1[k - 1], 'rx', shift(k))  4.02 us
    ppermute x1, starting transfers between devices, per_device(): lax.ppermute(send0[1], 'ry', shift(-2))  3.8 us
  transfers between devices with their start and end apart: 18, of which 7 were waited for; matrix products, arithmetic and copies ran while one was open for 0% of the time, Pallas kernels for 44%

profile of v4, /device:TPU:130, one launch (start us, length us, event | category | flops | bytes accessed | tf_op | source)
XLA Modules:
  0.0 93.1 jit_solution(17150739830464406239)
XLA Ops:
  2.6 3.3 %prep.1 = (bf16[128,2688]{1,0:T(8,128)(2,1)S(1)}, bf16[128,2688]{1,0:T(8,128)(2,1)S(1)}, bf16[128,2688]{1,0:T(8,128)(2,1)S(1)}, bf16[128,2688]{1,0:T(8,128)(2,1)...) custom-call(s32[1]{0:T(128)} %bitcast.1.x_idx, ...), custom_call_target="tpu_custom_call" | custom-call | flops 1000 | bytes 1000 | tf_op jit(solution)/shard_map/prep/pallas_call | solution.py:154
  5.8 1.6 %collective-permute-start.1 = (bf16[128,2688]{1,0:T(8,128)(2,1)S(1)}, bf16[128,2688]{1,0:T(8,128)(2,1)S(1)}, u32[]{:S(2)}, u32[]{:S(2)}) collective-permute-start(bf16[128,2688]{1,0:T(8,128)(2,1)S(1)} %get-tuple-element.91), channel_id=1, source_target_pairs={{0,4},{4,8},{8,12},{12,0},{1,5},{5,9},{9,13},{13,1},{2,6},{6,10},{... | collective-permute-start | bytes 2064392 | tf_op jit(solution)/shard_map/ppermute | solution.py:416
  7.4 1.1 %collective-permute-start.2 = (bf16[128,2688]{1,0:T(8,128)(2,1)S(1)}, bf16[128,2688]{1,0:T(8,128)(2,1)S(1)}, u32[]{:S(2)}, u32[]{:S(2)}) collective-permute-start(bf16[128,2688]{1,0:T(8,128)(2,1)S(1)} %get-tuple-element.92), channel_id=1, source_target_pairs={{0,8},{4,12},{8,0},{12,4},{1,9},{5,13},{9,1},{13,5},{2,10},{6,14},... | collective-permute-start | bytes 2064392 | tf_op jit(solution)/shard_map/ppermute | solution.py:416
  8.5 2.2 %collective-permute-start.3 = (bf16[128,2688]{1,0:T(8,128)(2,1)S(1)}, bf16[128,2688]{1,0:T(8,128)(2,1)S(1)}, u32[]{:S(2)}, u32[]{:S(2)}) collective-permute-start(bf16[128,2688]{1,0:T(8,128)(2,1)S(1)} %get-tuple-element.93), channel_id=1, source_target_pairs={{0,12},{4,0},{8,4},{12,8},{1,13},{5,1},{9,5},{13,9},{2,14},{6,2},{... | collective-permute-start | bytes 2064392 | tf_op jit(solution)/shard_map/ppermute | solution.py:416
  10.7 3.2 %collective-permute-start = (bf16[1040,256]{1,0:T(8,128)(2,1)S(1)}, bf16[1040,256]{1,0:T(8,128)(2,1)S(1)}, u32[]{:S(2)}, u32[]{:S(2)}) collective-permute-start(bf16[1040,256]{1,0:T(8,128)(2,1)S(1)} %get-tuple-element.94.refs_12_.refs_16_.refs_8_), channel_id=1, source_target_pairs={{0,2},{1,3},{2,0},{3,1},{4,6},{5,7},{6,4},{7,5},{8,10},{9,11},{10,... | collective-permute-start | bytes 1597448 | tf_op jit(solution)/shard_map/ppermute | solution.py:419
  13.9 13.5 %within0.1 = (bf16[1,128,2048]{2,1,0:T(8,128)(2,1)}, f32[128,2048]{1,0:T(8,128)S(1)}, f32[4,128,128]{2,1,0:T(8,128)S(1)}, f32[4,128,128]{2,1,0:T(8,128)S(1)}) custom-call(bf16[1,128,16384]{2,1,0:T(8,128)(2,1)} %x_ref.5, bf16[1,128,16384]{2,1,0:T(8,128)(2,1)} %cot_ref.5, bf16[1,128,2048]{2,1,0:T(8,128)(2,1)} %b_ref.5, bf16[1,128,2048]{2,1,0:T(8,128)(2,1)} %c_ref.5, ...), custom_call_target="tpu_custom_call" | custom-call | flops 1000 | bytes 1000 | tf_op jit(solution)/shard_map/within0/pallas_call | solution.py:233
  27.4 0.0 collective-permute-done.refs_14_.refs_18_
  27.4 1.1 %collective-permute-start.5 = (bf16[1040,256]{1,0:T(8,128)(2,1)S(1)}, bf16[1040,256]{1,0:T(8,128)(2,1)S(1)}, u32[]{:S(2)}, u32[]{:S(2)}) collective-permute-start(bf16[1040,256]{1,0:T(8,128)(2,1)S(1)} %get-tuple-element.94.refs_12_.refs_16_.refs_8_), channel_id=1, source_target_pairs={{0,3},{1,0},{2,1},{3,2},{4,7},{5,4},{6,5},{7,6},{8,11},{9,8},{10,9... | collective-permute-start | bytes 1597448 | tf_op jit(solution)/shard_map/ppermute | solution.py:422
  28.4 1.0 %collective-permute-start.4 = (bf16[1040,256]{1,0:T(8,128)(2,1)S(1)}, bf16[1040,256]{1,0:T(8,128)(2,1)S(1)}, u32[]{:S(2)}, u32[]{:S(2)}) collective-permute-start(bf16[1040,256]{1,0:T(8,128)(2,1)S(1)} %get-tuple-element.94.refs_12_.refs_16_.refs_8_), channel_id=1, source_target_pairs={{0,1},{1,2},{2,3},{3,0},{4,5},{5,6},{6,7},{7,4},{8,9},{9,10},{10,1... | collective-permute-start | bytes 1597448 | tf_op jit(solution)/shard_map/ppermute | solution.py:422
  29.4 7.7 %within4.1 = (bf16[1,128,2048]{2,1,0:T(8,128)(2,1)}, f32[128,2048]{1,0:T(8,128)S(1)}, f32[4,128,128]{2,1,0:T(8,128)S(1)}, f32[4,128,128]{2,1,0:T(8,128)S(1)}) custom-call(bf16[1,128,16384]{2,1,0:T(8,128)(2,1)} %x_ref.5, bf16[1,128,16384]{2,1,0:T(8,128)(2,1)} %cot_ref.5, ...), custom_call_target="tpu_custom_call", output_to_operand_aliasing={{0}: (6, {}), {1}: (7, {}), {2}: (8, {}), {3}: (9, {})} | custom-call | flops 1000 | bytes 1000 | tf_op jit(solution)/shard_map/within4/pallas_call | solution.py:233
  37.1 0.0 collective-permute-done.1.refs_1_.refs_5_.refs_9_
  37.1 0.0 collective-permute-start.6
  37.1 0.0 collective-permute-done.2.refs_2_.refs_6_.refs_10_
  37.1 3.5 %collective-permute-start.7 = (bf16[128,2048]{1,0:T(8,128)(2,1)S(1)}, bf16[128,2048]{1,0:T(8,128)(2,1)S(1)}, u32[]{:S(2)}, u32[]{:S(2)}) collective-permute-start(bf16[128,2048]{1,0:T(8,128)(2,1)S(1)} %get-tuple-element.109), channel_id=1, source_target_pairs={{0,8},{4,12},{8,0},{12,4},{1,9},{5,13},{9,1},{13,5},{2,10},{6,14},... | collective-permute-start | bytes 1572872 | tf_op jit(solution)/shard_map/ppermute | solution.py:425
  40.6 0.0 collective-permute-done.3.refs_3_.refs_7_.refs_11_
  40.6 1.1 %collective-permute-start.8 = (bf16[128,2048]{1,0:T(8,128)(2,1)S(1)}, bf16[128,2048]{1,0:T(8,128)(2,1)S(1)}, u32[]{:S(2)}, u32[]{:S(2)}) collective-permute-start(bf16[128,2048]{1,0:T(8,128)(2,1)S(1)} %get-tuple-element.110), channel_id=1, source_target_pairs={{0,12},{4,0},{8,4},{12,8},{1,13},{5,1},{9,5},{13,9},{2,14},{6,2},{... | collective-permute-start | bytes 1572872 | tf_op jit(solution)/shard_map/ppermute | solution.py:425
  41.7 0.0 collective-permute-done.5.refs_15_.refs_19_
  41.7 0.3 collective-permute-done.4.refs_13_.refs_17_
  42.1 5.3 %owner0.1 = (f32[256,512]{1,0:T(8,128)S(1)}, s16[272,512]{1,0:T(8,128)(2,1)S(1)}, s16[272,512]{1,0:T(8,128)(2,1)S(1)}, s16[272,512]{1,0:T(8,128)(2,1)S(1)}, f32[...) custom-call(s32[1]{0:T(128)} %bitcast.y_idx, ...), custom_call_target="tpu_custom_call" | custom-call | flops 1000 | bytes 1000 | tf_op jit(solution)/shard_map/owner0/pallas_call | solution.py:307
  47.4 3.8 %collective-permute-start.10 = (s16[272,512]{1,0:T(8,128)(2,1)S(1)}, s16[272,512]{1,0:T(8,128)(2,1)S(1)}, u32[]{:S(2)}, u32[]{:S(2)}) collective-permute-start(s16[272,512]{1,0:T(8,128)(2,1)S(1)} %get-tuple-element.112), channel_id=1, source_target_pairs={{0,2},{1,3},{2,0},{3,1},{4,6},{5,7},{6,4},{7,5},{8,10},{9,11},{10,... | collective-permute-start | bytes 835592 | tf_op jit(solution)/shard_map/ppermute | solution.py:428
  51.2 0.2 collective-permute-start.11
  51.3 7.7 %within6.1 = (bf16[1,128,2048]{2,1,0:T(8,128)(2,1)}, f32[128,2048]{1,0:T(8,128)S(1)}, f32[4,128,128]{2,1,0:T(8,128)S(1)}, f32[4,128,128]{2,1,0:T(8,128)S(1)}) custom-call(bf16[1,128,16384]{2,1,0:T(8,128)(2,1)} %x_ref.5, bf16[1,128,16384]{2,1,0:T(8,128)(2,1)} %cot_ref.5, ...), custom_call_target="tpu_custom_call", output_to_operand_aliasing={{0}: (6, {}), {1}: (7, {}), {2}: (8, {}), {3}: (9, {})} | custom-call | flops 1000 | bytes 1000 | tf_op jit(solution)/shard_map/within6/pallas_call | solution.py:233
  59.1 0.0 collective-permute-done.6.refs_1_
  59.1 0.0 collective-permute-done.7.refs_2_
  59.1 4.0 %collective-permute-done.8.refs_3_ = bf16[128,2048]{1,0:T(8,128)(2,1)S(1)} collective-permute-done((bf16[128,2048]{1,0:T(8,128)(2,1)S(1)}, bf16[128,2048]{1,0:T(8,128)(2,1)S(1)}, u32[]{:S(2)}, u32[]{:S(2)}) %collective-permute-start.8) | collective-permute-done | bytes 524320 | tf_op jit(solution)/shard_map/ppermute | solution.py:425
  63.1 2.9 %collective-permute-start.9 = (s16[272,512]{1,0:T(8,128)(2,1)S(1)}, s16[272,512]{1,0:T(8,128)(2,1)S(1)}, u32[]{:S(2)}, u32[]{:S(2)}) collective-permute-start(s16[272,512]{1,0:T(8,128)(2,1)S(1)} %get-tuple-element.111), channel_id=1, source_target_pairs={{0,3},{1,0},{2,1},{3,2},{4,7},{5,4},{6,5},{7,6},{8,11},{9,8},{10,9... | collective-permute-start | bytes 835592 | tf_op jit(solution)/shard_map/ppermute | solution.py:433
  66.0 0.0 collective-permute-done.10.refs_2_
  66.0 0.0 collective-permute-done.11.refs_3_
  66.0 0.0 copy-start
  66.0 0.0 copy-start.1
  66.0 5.3 %owner1.1 = (f32[256,512]{1,0:T(8,128)S(1)}, s16[272,512]{1,0:T(8,128)(2,1)S(1)}, s16[272,512]{1,0:T(8,128)(2,1)S(1)}, s16[272,512]{1,0:T(8,128)(2,1)S(1)}, f32[...) custom-call(s32[1]{0:T(128)} %bitcast.y_idx, ...), custom_call_target="tpu_custom_call" | custom-call | flops 1000 | bytes 1000 | tf_op jit(solution)/shard_map/owner1/pallas_call | solution.py:307
  71.3 0.6 collective-permute-done.9.refs_1_
  71.9 1.7 %collective-permute-start.12 = (f32[144,512]{1,0:T(8,128)S(1)}, f32[144,512]{1,0:T(8,128)S(1)}, u32[]{:S(2)}, u32[]{:S(2)}) collective-permute-start(f32[144,512]{1,0:T(8,128)S(1)} %get-tuple-element.136), channel_id=1, source_target_pairs={{0,8},{4,12},{8,0},{12,4},{1,9},{5,13},{9,1},{13,5},{2,10},{6,14},... | collective-permute-start | bytes 884744 | tf_op jit(solution)/shard_map/ppermute | solution.py:437
  73.7 0.6 collective-permute-start.13
  74.2 1.4 %collective-permute-start.14 = (f32[144,512]{1,0:T(8,128)S(1)}, f32[144,512]{1,0:T(8,128)S(1)}, u32[]{:S(2)}, u32[]{:S(2)}) collective-permute-start(f32[144,512]{1,0:T(8,128)S(1)} %get-tuple-element.138), channel_id=1, source_target_pairs={{0,4},{4,8},{8,12},{12,0},{1,5},{5,9},{9,13},{13,1},{2,6},{6,10},{... | collective-permute-start | bytes 884744 | tf_op jit(solution)/shard_map/ppermute | solution.py:437
  75.7 2.3 %collective-permute-start.15 = (s16[272,512]{1,0:T(8,128)(2,1)S(1)}, s16[272,512]{1,0:T(8,128)(2,1)S(1)}, u32[]{:S(2)}, u32[]{:S(2)}) collective-permute-start(s16[272,512]{1,0:T(8,128)(2,1)S(1)} %get-tuple-element.142), channel_id=1, source_target_pairs={{0,2},{1,3},{2,0},{3,1},{4,6},{5,7},{6,4},{7,5},{8,10},{9,11},{10,... | collective-permute-start | bytes 835592 | tf_op jit(solution)/shard_map/ppermute | solution.py:438
  78.0 1.2 %collective-permute-start.16 = (s16[272,512]{1,0:T(8,128)(2,1)S(1)}, s16[272,512]{1,0:T(8,128)(2,1)S(1)}, u32[]{:S(2)}, u32[]{:S(2)}) collective-permute-start(s16[272,512]{1,0:T(8,128)(2,1)S(1)} %get-tuple-element.143), channel_id=1, source_target_pairs={{0,3},{1,0},{2,1},{3,2},{4,7},{5,4},{6,5},{7,6},{8,11},{9,8},{10,9... | collective-permute-start | bytes 835592 | tf_op jit(solution)/shard_map/ppermute | solution.py:438
  79.2 4.2 %collective-permute-done.12.r1 = f32[144,512]{1,0:T(8,128)S(1)} collective-permute-done((f32[144,512]{1,0:T(8,128)S(1)}, f32[144,512]{1,0:T(8,128)S(1)}, u32[]{:S(2)}, u32[]{:S(2)}) %collective-permute-start.12) | collective-permute-done | bytes 294944 | tf_op jit(solution)/shard_map/ppermute | solution.py:437
  83.4 1.0 %collective-permute-start.17 = (s16[272,512]{1,0:T(8,128)(2,1)S(1)}, s16[272,512]{1,0:T(8,128)(2,1)S(1)}, u32[]{:S(2)}, u32[]{:S(2)}) collective-permute-start(s16[272,512]{1,0:T(8,128)(2,1)S(1)} %get-tuple-element.144), channel_id=1, source_target_pairs={{0,1},{1,2},{2,3},{3,0},{4,5},{5,6},{6,7},{7,4},{8,9},{9,10},{10,1... | collective-permute-start | bytes 835592 | tf_op jit(solution)/shard_map/ppermute | solution.py:438
  84.4 3.3 %collective-permute-done.13.r2 = f32[144,512]{1,0:T(8,128)S(1)} collective-permute-done((f32[144,512]{1,0:T(8,128)S(1)}, f32[144,512]{1,0:T(8,128)S(1)}, u32[]{:S(2)}, u32[]{:S(2)}) %collective-permute-start.13) | collective-permute-done | bytes 294944 | tf_op jit(solution)/shard_map/ppermute | solution.py:437
  87.8 0.0 collective-permute-done.14.r3
  87.8 0.0 copy-done
  87.8 0.0 copy-done.1
  87.8 1.3 %tokens.1 = (bf16[1,128,2048]{2,1,0:T(8,128)(2,1)}, f32[1,128,256]{2,1,0:T(8,128)}) custom-call(s32[1]{0:T(128)} %bitcast.1.x_idx, f32[1,128,256]{2,1,0:T(8,128)S(1)} %copy-done, f32[1,256]{1,0:T(1,128)S(1)} %bitcast.6, f32[128,2048]{1,0:T(8,128)S(1)} %get-tuple-element.132.gc_ref, f32[4,128,128]{2,1,0:T(8,128)S(1)} %get-tuple-element.133.q_ref, ...), custom_call_target="tpu_custom_call" | custom-call | flops 1000 | bytes 1000 | tf_op jit(solution)/shard_map/tokens/pallas_call | solution.py:355
  89.1 0.0 collective-permute-done.15.refs_5_
  89.1 1.8 %collective-permute-done.16.refs_6_ = s16[272,512]{1,0:T(8,128)(2,1)S(1)} collective-permute-done((s16[272,512]{1,0:T(8,128)(2,1)S(1)}, s16[272,512]{1,0:T(8,128)(2,1)S(1)}, u32[]{:S(2)}, u32[]{:S(2)}) %collective-permute-start.16) | collective-permute-done | bytes 278560 | tf_op jit(solution)/shard_map/ppermute | solution.py:438
  90.9 0.7 collective-permute-done.17.refs_7_
  91.6 1.5 %state_out.1 = f32[1024,256]{1,0:T(8,128)} custom-call(f32[256,512]{1,0:T(8,128)S(1)} %get-tuple-element.96.refs_0_, s16[272,512]{1,0:T(8,128)(2,1)S(1)} %collective-permute-done.9.refs_1_, s16[272,512]{1,0:T(8,128)(2,1)S(1)} %collective-permute-done.10.refs_2_, s16[272,512]{1,0:T(8,128)(2,1)S(1)} %collective-permute-done.11.refs_3_, ...), custom_call_target="tpu_custom_call" | custom-call | flops 1000 | bytes 1000 | tf_op jit(solution)/shard_map/state_out/pallas_call | solution.py:387
Async XLA Ops:
  5.8 31.3 %collective-permute-start.1 = (bf16[128,2688]{1,0:T(8,128)(2,1)S(1)}, bf16[128,2688]{1,0:T(8,128)(2,1)S(1)}, u32[]{:S(2)}, u32[]{:S(2)}) collective-permute-start(bf16[128,2688]{1,0:T(8,128)(2,1)S(1)} %get-tuple-element.91), channel_id=1, source_target_pairs={{0,4},{4,8},{8,12},{12,0},{1,5},{5,9},{9,13},{13,1},{2,6},{6,10},{... | collective-permute-start | bytes 2064392 | tf_op jit(solution)/shard_map/ppermute | solution.py:416
  7.4 29.7 %collective-permute-start.2 = (bf16[128,2688]{1,0:T(8,128)(2,1)S(1)}, bf16[128,2688]{1,0:T(8,128)(2,1)S(1)}, u32[]{:S(2)}, u32[]{:S(2)}) collective-permute-start(bf16[128,2688]{1,0:T(8,128)(2,1)S(1)} %get-tuple-element.92), channel_id=1, source_target_pairs={{0,8},{4,12},{8,0},{12,4},{1,9},{5,13},{9,1},{13,5},{2,10},{6,14},... | collective-permute-start | bytes 2064392 | tf_op jit(solution)/shard_map/ppermute | solution.py:416
  8.5 32.1 %collective-permute-start.3 = (bf16[128,2688]{1,0:T(8,128)(2,1)S(1)}, bf16[128,2688]{1,0:T(8,128)(2,1)S(1)}, u32[]{:S(2)}, u32[]{:S(2)}) collective-permute-start(bf16[128,2688]{1,0:T(8,128)(2,1)S(1)} %get-tuple-element.93), channel_id=1, source_target_pairs={{0,12},{4,0},{8,4},{12,8},{1,13},{5,1},{9,5},{13,9},{2,14},{6,2},{... | collective-permute-start | bytes 2064392 | tf_op jit(solution)/shard_map/ppermute | solution.py:416
  10.7 16.7 %collective-permute-start = (bf16[1040,256]{1,0:T(8,128)(2,1)S(1)}, bf16[1040,256]{1,0:T(8,128)(2,1)S(1)}, u32[]{:S(2)}, u32[]{:S(2)}) collective-permute-start(bf16[1040,256]{1,0:T(8,128)(2,1)S(1)} %get-tuple-element.94.refs_12_.refs_16_.refs_8_), channel_id=1, source_target_pairs={{0,2},{1,3},{2,0},{3,1},{4,6},{5,7},{6,4},{7,5},{8,10},{9,11},{10,... | collective-permute-start | bytes 1597448 | tf_op jit(solution)/shard_map/ppermute | solution.py:419
  27.4 14.4 %collective-permute-start.5 = (bf16[1040,256]{1,0:T(8,128)(2,1)S(1)}, bf16[1040,256]{1,0:T(8,128)(2,1)S(1)}, u32[]{:S(2)}, u32[]{:S(2)}) collective-permute-start(bf16[1040,256]{1,0:T(8,128)(2,1)S(1)} %get-tuple-element.94.refs_12_.refs_16_.refs_8_), channel_id=1, source_target_pairs={{0,3},{1,0},{2,1},{3,2},{4,7},{5,4},{6,5},{7,6},{8,11},{9,8},{10,9... | collective-permute-start | bytes 1597448 | tf_op jit(solution)/shard_map/ppermute | solution.py:422
  28.4 13.7 %collective-permute-start.4 = (bf16[1040,256]{1,0:T(8,128)(2,1)S(1)}, bf16[1040,256]{1,0:T(8,128)(2,1)S(1)}, u32[]{:S(2)}, u32[]{:S(2)}) collective-permute-start(bf16[1040,256]{1,0:T(8,128)(2,1)S(1)} %get-tuple-element.94.refs_12_.refs_16_.refs_8_), channel_id=1, source_target_pairs={{0,1},{1,2},{2,3},{3,0},{4,5},{5,6},{6,7},{7,4},{8,9},{9,10},{10,1... | collective-permute-start | bytes 1597448 | tf_op jit(solution)/shard_map/ppermute | solution.py:422
  37.1 21.9 %collective-permute-start.6 = (bf16[128,2048]{1,0:T(8,128)(2,1)S(1)}, bf16[128,2048]{1,0:T(8,128)(2,1)S(1)}, u32[]{:S(2)}, u32[]{:S(2)}) collective-permute-start(bf16[128,2048]{1,0:T(8,128)(2,1)S(1)} %get-tuple-element.108), channel_id=1, source_target_pairs={{0,4},{4,8},{8,12},{12,0},{1,5},{5,9},{9,13},{13,1},{2,6},{6,10},{... | collective-permute-start | bytes 1572872 | tf_op jit(solution)/shard_map/ppermute | solution.py:425
  37.1 21.9 %collective-permute-start.7 = (bf16[128,2048]{1,0:T(8,128)(2,1)S(1)}, bf16[128,2048]{1,0:T(8,128)(2,1)S(1)}, u32[]{:S(2)}, u32[]{:S(2)}) collective-permute-start(bf16[128,2048]{1,0:T(8,128)(2,1)S(1)} %get-tuple-element.109), channel_id=1, source_target_pairs={{0,8},{4,12},{8,0},{12,4},{1,9},{5,13},{9,1},{13,5},{2,10},{6,14},... | collective-permute-start | bytes 1572872 | tf_op jit(solution)/shard_map/ppermute | solution.py:425
  40.6 22.5 %collective-permute-start.8 = (bf16[128,2048]{1,0:T(8,128)(2,1)S(1)}, bf16[128,2048]{1,0:T(8,128)(2,1)S(1)}, u32[]{:S(2)}, u32[]{:S(2)}) collective-permute-start(bf16[128,2048]{1,0:T(8,128)(2,1)S(1)} %get-tuple-element.110), channel_id=1, source_target_pairs={{0,12},{4,0},{8,4},{12,8},{1,13},{5,1},{9,5},{13,9},{2,14},{6,2},{... | collective-permute-start | bytes 1572872 | tf_op jit(solution)/shard_map/ppermute | solution.py:425
  47.4 18.6 %collective-permute-start.10 = (s16[272,512]{1,0:T(8,128)(2,1)S(1)}, s16[272,512]{1,0:T(8,128)(2,1)S(1)}, u32[]{:S(2)}, u32[]{:S(2)}) collective-permute-start(s16[272,512]{1,0:T(8,128)(2,1)S(1)} %get-tuple-element.112), channel_id=1, source_target_pairs={{0,2},{1,3},{2,0},{3,1},{4,6},{5,7},{6,4},{7,5},{8,10},{9,11},{10,... | collective-permute-start | bytes 835592 | tf_op jit(solution)/shard_map/ppermute | solution.py:428
  51.2 14.8 %collective-permute-start.11 = (s16[272,512]{1,0:T(8,128)(2,1)S(1)}, s16[272,512]{1,0:T(8,128)(2,1)S(1)}, u32[]{:S(2)}, u32[]{:S(2)}) collective-permute-start(s16[272,512]{1,0:T(8,128)(2,1)S(1)} %get-tuple-element.113), channel_id=1, source_target_pairs={{0,1},{1,2},{2,3},{3,0},{4,5},{5,6},{6,7},{7,4},{8,9},{9,10},{10,1... | collective-permute-start | bytes 835592 | tf_op jit(solution)/shard_map/ppermute | solution.py:428
  63.1 8.8 %collective-permute-start.9 = (s16[272,512]{1,0:T(8,128)(2,1)S(1)}, s16[272,512]{1,0:T(8,128)(2,1)S(1)}, u32[]{:S(2)}, u32[]{:S(2)}) collective-permute-start(s16[272,512]{1,0:T(8,128)(2,1)S(1)} %get-tuple-element.111), channel_id=1, source_target_pairs={{0,3},{1,0},{2,1},{3,2},{4,7},{5,4},{6,5},{7,6},{8,11},{9,8},{10,9... | collective-permute-start | bytes 835592 | tf_op jit(solution)/shard_map/ppermute | solution.py:433
  66.0 21.8 %copy-start = (f32[1,128,256]{2,1,0:T(8,128)S(1)}, f32[1,128,256]{2,1,0:T(8,128)}, u32[]{:S(2)}) copy-start(f32[1,128,256]{2,1,0:T(8,128)} %dt_ref.1) | copy-start | bytes 393220
  66.0 21.8 %copy-start.1 = (f32[256]{0:T(256)S(1)}, f32[256]{0:T(256)}, u32[]{:S(2)}) copy-start(f32[256]{0:T(256)} %param.16) | copy-start | bytes 3076
  71.9 11.5 %collective-permute-start.12 = (f32[144,512]{1,0:T(8,128)S(1)}, f32[144,512]{1,0:T(8,128)S(1)}, u32[]{:S(2)}, u32[]{:S(2)}) collective-permute-start(f32[144,512]{1,0:T(8,128)S(1)} %get-tuple-element.136), channel_id=1, source_target_pairs={{0,8},{4,12},{8,0},{12,4},{1,9},{5,13},{9,1},{13,5},{2,10},{6,14},... | collective-permute-start | bytes 884744 | tf_op jit(solution)/shard_map/ppermute | solution.py:437
  73.7 14.1 %collective-permute-start.13 = (f32[144,512]{1,0:T(8,128)S(1)}, f32[144,512]{1,0:T(8,128)S(1)}, u32[]{:S(2)}, u32[]{:S(2)}) collective-permute-start(f32[144,512]{1,0:T(8,128)S(1)} %get-tuple-element.137), channel_id=1, source_target_pairs={{0,12},{4,0},{8,4},{12,8},{1,13},{5,1},{9,5},{13,9},{2,14},{6,2},{... | collective-permute-start | bytes 884744 | tf_op jit(solution)/shard_map/ppermute | solution.py:437
  74.2 13.5 %collective-permute-start.14 = (f32[144,512]{1,0:T(8,128)S(1)}, f32[144,512]{1,0:T(8,128)S(1)}, u32[]{:S(2)}, u32[]{:S(2)}) collective-permute-start(f32[144,512]{1,0:T(8,128)S(1)} %get-tuple-element.138), channel_id=1, source_target_pairs={{0,4},{4,8},{8,12},{12,0},{1,5},{5,9},{9,13},{13,1},{2,6},{6,10},{... | collective-permute-start | bytes 884744 | tf_op jit(solution)/shard_map/ppermute | solution.py:437
  75.7 13.4 %collective-permute-start.15 = (s16[272,512]{1,0:T(8,128)(2,1)S(1)}, s16[272,512]{1,0:T(8,128)(2,1)S(1)}, u32[]{:S(2)}, u32[]{:S(2)}) collective-permute-start(s16[272,512]{1,0:T(8,128)(2,1)S(1)} %get-tuple-element.142), channel_id=1, source_target_pairs={{0,2},{1,3},{2,0},{3,1},{4,6},{5,7},{6,4},{7,5},{8,10},{9,11},{10,... | collective-permute-start | bytes 835592 | tf_op jit(solution)/shard_map/ppermute | solution.py:438
  78.0 12.9 %collective-permute-start.16 = (s16[272,512]{1,0:T(8,128)(2,1)S(1)}, s16[272,512]{1,0:T(8,128)(2,1)S(1)}, u32[]{:S(2)}, u32[]{:S(2)}) collective-permute-start(s16[272,512]{1,0:T(8,128)(2,1)S(1)} %get-tuple-element.143), channel_id=1, source_target_pairs={{0,3},{1,0},{2,1},{3,2},{4,7},{5,4},{6,5},{7,6},{8,11},{9,8},{10,9... | collective-permute-start | bytes 835592 | tf_op jit(solution)/shard_map/ppermute | solution.py:438
  83.4 8.2 %collective-permute-start.17 = (s16[272,512]{1,0:T(8,128)(2,1)S(1)}, s16[272,512]{1,0:T(8,128)(2,1)S(1)}, u32[]{:S(2)}, u32[]{:S(2)}) collective-permute-start(s16[272,512]{1,0:T(8,128)(2,1)S(1)} %get-tuple-element.144), channel_id=1, source_target_pairs={{0,1},{1,2},{2,3},{3,0},{4,5},{5,6},{6,7},{7,4},{8,9},{9,10},{10,1... | collective-permute-start | bytes 835592 | tf_op jit(solution)/shard_map/ppermute | solution.py:438
